TPU v7x, 32 devices: a whole 2x2x4 slice. The times are simulated.
32 devices in a mesh: grp: 2 (over x), seq: 16 (over z, y, core).
Axes of the slice: x: 2, y: 2, z: 4, core: 2. Of those that a mesh axis runs over, the one named last changes fastest.
Arguments:
- tokens: bfloat16 [16384, 1024], P(('grp', 'seq')), parts along dimension 0, may hold values from -6 to 6
- value_weight: bfloat16 [1024, 1024], replicated, may hold values from -0.1875 to 0.1875
- gate_weight: bfloat16 [1024, 1024], replicated, may hold values from -0.1875 to 0.1875
- out_weight: bfloat16 [1024, 1024], replicated, may hold values from -0.1875 to 0.1875
- kernel_weight: bfloat16 [1024, 16], replicated, may hold values from -0.1875 to 0.1875
- kernel_bias: float32 [16], replicated, may hold values from -4 to 4
Outputs:
- mixed: bfloat16 [16384, 1024], P(('grp', 'seq')), parts along dimension 0
There are 2 independent parts, one for each index of `grp`. A program takes and returns all parts, laid end to end along the dimension named above; an argument that names none is the same for every part. Nothing has to cross between parts.
All inputs are finite; a program needn't handle non-finite values.
Results may differ from a plain program's by a relative error of at most 0.0071.
Values may be sent and summed in bfloat16 or wider, within the bound.
No kernel may reach another device: no remote copies, remote signals or barrier semaphores. Data moves between devices by JAX's collectives and lax.ppermute only.
A program may use at most 128 MiB of HBM per device.

v0:
```python
import functools

import jax
import jax.numpy as jnp
from jax import lax
from jax.experimental import pallas as pl
from jax.experimental.pallas import tpu as pltpu
from jax.sharding import PartitionSpec as P

f32 = jnp.float32
bf16 = jnp.bfloat16
LANES = 128
TILE = 16
VMEM = pl.BlockSpec(memory_space=pltpu.VMEM)
PARAMS = pltpu.CompilerParams(vmem_limit_bytes=48 * 2**20)
LARGE = pltpu.CompilerParams(vmem_limit_bytes=62 * 2**20)


def cost(flops, nbytes):
    return pl.CostEstimate(flops=int(flops), bytes_accessed=int(nbytes), transcendentals=0)


def whole_block(shape):
    return pl.BlockSpec(shape, lambda i: (0,) * len(shape))


def shape_of(shape, dtype=bf16):
    return jax.ShapeDtypeStruct(shape, dtype)


def place():
    me = lax.axis_index("seq")
    return me // 2, lax.rem(me, 2)


def project_body(sizes, tokens, weight, lag_weight, lag_bias, *refs):
    devices, per, first, heads, rows = sizes
    out, lag_rows = refs[0], refs[-1]
    at = pl.program_id(0)
    count = weight.shape[1] // per
    tiles = rows // LANES

    @pl.when(at == 0)
    def _():
        logits = lax.dot_general(
            lag_weight[...], tokens[...], (((1,), (1,)), ((), ())), preferred_element_type=f32
        ) + lag_bias[...]
        lag_rows[...] = jnp.tanh(logits) * (rows * devices) ** (-0.5)

    part = jnp.dot(tokens[...], weight[...], preferred_element_type=f32).astype(bf16).T
    for group in range(count):
        block = part[per * group : per * group + first]
        for tile in range(tiles):
            out[group, first * tile : first * tile + first] = block[:, LANES * tile : LANES * tile + LANES]
        head = (at * count + group) * heads // devices
        row = lag_rows[pl.ds(head, 1), :]
        pieces = [row[:, LANES * tile : LANES * tile + LANES] for tile in range(tiles)]
        pieces.append(jnp.zeros((out.shape[1] - first * tiles - tiles, LANES), f32))
        out[group, first * tiles :] = jnp.concatenate(pieces, axis=0).astype(bf16)
    if first < per:
        keep, other = refs[1:3]
        chip, core = place()
        for pair in range(count // 2):
            low = part[per * 2 * pair + first : per * (2 * pair + 1)]
            high = part[per * (2 * pair + 1) + first : per * (2 * pair + 2)]
            slot = jnp.bitwise_xor(chip, at * (count // 2) + pair)
            keep[slot] = jnp.where(core == 0, low, high)
            other[slot] = jnp.where(core == 0, high, low)


def project(tokens, weight, lag_weight, lag_bias, devices, first):
    rows, width = tokens.shape
    heads = lag_weight.shape[1]
    per = width // devices
    step = max(2 * per, min(width, 256))
    count = step // per
    tall = first * (rows // LANES) + TILE
    outs = [shape_of((devices, tall, LANES))]
    specs = [pl.BlockSpec((count, tall, LANES), lambda i: (i, 0, 0))]
    if first < per:
        rest = (devices // 2, per - first, rows)
        outs += [shape_of(rest)] * 2
        specs += [whole_block(rest)] * 2
    return pl.pallas_call(
        functools.partial(project_body, (devices, per, first, heads, rows)),
        grid=(width // step,),
        out_shape=outs,
        in_specs=[
            whole_block((rows, width)),
            pl.BlockSpec((width, step), lambda i: (0, i)),
            whole_block((heads, width)),
            whole_block((heads, 1)),
        ],
        out_specs=specs,
        scratch_shapes=[pltpu.VMEM((heads, rows), f32)],
        compiler_params=LARGE,
        cost_estimate=cost(2 * rows * width * width, 4 * rows * width + 2 * width * width),
        name="project",
    )(tokens, weight, lag_weight.T, lag_bias.reshape(heads, 1))


def gate_body(tokens, weight, *refs):
    gate = jnp.dot(tokens[...], weight[...], preferred_element_type=f32)
    if len(refs) == 1:
        refs[0][...] = (gate / (1.0 + jnp.exp(-gate))).T
        return
    keep, other, out, *messages = refs
    out[...] = (gate / (1.0 + jnp.exp(-gate))).T

    @pl.when(pl.program_id(0) == 0)
    def _():
        for slot, message in enumerate(messages):
            message[0] = keep[slot]
            message[1] = other[slot]


def gate_columns(tokens, weight, pair):
    rows, width = tokens.shape
    step = min(width, 256)
    outs, out_specs, ins = [shape_of((width, rows), f32)], [pl.BlockSpec((step, rows), lambda i: (i, 0))], []
    if pair:
        chips, channels, _ = pair[0].shape
        outs += [shape_of((2, channels, rows))] * chips
        out_specs += [whole_block((2, channels, rows))] * chips
        ins = [whole_block(pair[0].shape)] * 2
    return pl.pallas_call(
        gate_body,
        grid=(width // step,),
        out_shape=outs,
        in_specs=[whole_block((rows, width)), pl.BlockSpec((width, step), lambda i: (0, i))] + ins,
        out_specs=out_specs,
        compiler_params=PARAMS,
        cost_estimate=cost(2 * rows * width * width, 4 * rows * width + 2 * width * width),
        name="gate",
    )(tokens, weight, *pair)


def fill_strips(row, plus, minus):
    length = row.shape[1]
    half = length // 2
    lead = plus.shape[1] - half
    low, high = row[:, :half] * 0.5, row[:, half:] * 0.5
    for ref, line, sign in ((plus, low + high, 1.0), (minus, low - high, -1.0)):
        for piece in range(LANES // TILE):
            turned = pltpu.roll(
                jnp.broadcast_to(line, (TILE, half)), TILE * piece, 1, stride=1, stride_axis=0
            )
            here = slice(TILE * piece, TILE * piece + TILE)
            edge = turned[:, :LANES]
            if sign < 0:
                down = lax.broadcasted_iota(jnp.int32, (TILE, LANES), 0) + TILE * piece
                across = lax.broadcasted_iota(jnp.int32, (TILE, LANES), 1)
                edge = jnp.where(across < down, -edge, edge)
            ref[here, :lead] = (turned[:, half - lead :] * sign).astype(bf16)
            ref[here, lead : lead + LANES] = edge.astype(bf16)
            ref[here, lead + LANES :] = turned[:, LANES:].astype(bf16)


def convolve(block_of, plus, minus, twice_plus, twice_minus, acc_plus, acc_minus):
    count, channels, span = twice_plus.shape
    half = count // 2
    lead = plus.shape[1] - half * span
    for at in range(half):
        low, high = block_of(at).astype(f32), block_of(at + half).astype(f32)
        total, gap = (low + high).astype(bf16), (low - high).astype(bf16)
        twice_plus[at] = total
        twice_plus[at + half] = total
        twice_minus[at] = -gap
        twice_minus[at + half] = gap
    group = min(half, 4)
    for acc, twice, strip in ((acc_plus, twice_plus, plus), (acc_minus, twice_minus, minus)):
        for start in range(0, half, group):
            left, right = [], []
            for lag in range(start, start + group):
                left.append(twice[half - lag : 2 * half - lag].reshape(half * channels, span))
                for part in range(span // LANES):
                    begin = span * lag + lead - LANES * part
                    right.append(strip[:, begin : begin + span])
            piece = jnp.dot(
                jnp.concatenate(left, axis=1), jnp.concatenate(right, axis=0), preferred_element_type=f32
            )
            acc[...] = piece if start == 0 else acc[...] + piece


def first_body(channels, values, *refs):
    out, plus, minus, *scratch = refs[-7:]
    count, tall, _ = values.shape
    span = out.shape[2]
    tiles = span // LANES
    pieces = []
    for at in range(count):
        rows = values[at, channels * tiles :].astype(f32)
        pieces += [rows[tile : tile + 1] for tile in range(tiles)]
    fill_strips(jnp.concatenate(pieces, axis=1), plus, minus)

    def block_of(at):
        return jnp.concatenate(
            [values[at, channels * tile : channels * tile + channels] for tile in range(tiles)], axis=1
        )

    convolve(block_of, plus, minus, *scratch)
    acc_plus, acc_minus = scratch[2:]
    half = count // 2
    out[:half] = (acc_plus[...] + acc_minus[...]).reshape(half, channels, span).astype(bf16)
    out[half:] = (acc_plus[...] - acc_minus[...]).reshape(half, channels, span).astype(bf16)


def scratch_for(count, channels, span):
    return [pltpu.VMEM((count, channels, span), bf16)] * 2 + [
        pltpu.VMEM((count // 2 * channels, span), f32)
    ] * 2


def convolve_first(values, channels, span, before):
    count = values.shape[0]
    strip = shape_of((LANES, count // 2 * span + span - LANES))
    return pl.pallas_call(
        functools.partial(first_body, channels),
        out_shape=[shape_of((count, channels, span)), strip, strip],
        in_specs=[VMEM] + [pl.BlockSpec(memory_space=pl.ANY)] * len(before),
        out_specs=[VMEM] * 3,
        scratch_shapes=scratch_for(count, channels, span),
        compiler_params=PARAMS,
        cost_estimate=cost(1e6, 1e5),
        name="conv_first",
    )(values, *before)


def rest_body(plus, minus, *refs):
    chips = (len(refs) - 7) // 1
    messages, keep, other, gathered = refs[:chips], refs[chips], refs[chips + 1], refs[chips + 2]
    scratch = refs[chips + 3 :]
    chip, core = place()
    for slot, message in enumerate(messages):
        base = 2 * jnp.bitwise_xor(chip, slot)
        gathered[base + core] = message[0]
        gathered[base + 1 - core] = message[1]
    convolve(lambda at: gathered[at], plus, minus, *scratch)
    acc_plus, acc_minus = scratch[2:]
    count, channels, span = gathered.shape
    half = count // 2
    gathered[:half] = (acc_plus[...] + acc_minus[...]).reshape(half, channels, span).astype(bf16)
    gathered[half:] = (acc_plus[...] - acc_minus[...]).reshape(half, channels, span).astype(bf16)
    for slot in range(chips):
        base = 2 * jnp.bitwise_xor(chip, slot)
        keep[slot] = gathered[base + core]
        other[slot] = gathered[base + 1 - core]


def convolve_rest(plus, minus, messages):
    chips = len(messages)
    _, channels, span = messages[0].shape
    result = shape_of((chips, channels, span))
    return pl.pallas_call(
        rest_body,
        out_shape=[result] * 2,
        in_specs=[VMEM] * (2 + chips),
        out_specs=[VMEM] * 2,
        scratch_shapes=[pltpu.VMEM((2 * chips, channels, span), bf16)]
        + scratch_for(2 * chips, channels, span),
        compiler_params=PARAMS,
        cost_estimate=cost(6e10, 1e8),
        name="conv_rest",
    )(plus, minus, *messages)


def join_body(keep, other, *messages):
    for slot, message in enumerate(messages):
        message[0] = keep[slot]
        message[1] = other[slot]


def join(keep, other):
    chips, channels, span = keep.shape
    return pl.pallas_call(
        join_body,
        out_shape=[shape_of((2, channels, span))] * chips,
        in_specs=[VMEM] * 2,
        out_specs=[VMEM] * chips,
        compiler_params=PARAMS,
        name="join",
    )(keep, other)


def mix_first_body(conv, gate, weight, out):
    devices, first, rows = conv.shape
    width = gate.shape[0]
    per = width // devices
    silu = gate[...].reshape(devices, per, rows)[:, :first]
    gated = (conv[...].astype(f32) * silu).astype(bf16).reshape(devices * first, rows)
    used = weight[...].reshape(devices, per, weight.shape[1])[:, :first]
    used = used.reshape(devices * first, weight.shape[1])
    out[...] = jnp.dot(gated.T, used, preferred_element_type=f32).astype(out.dtype)


def mix_first(conv, gate, weight, dtype):
    devices, first, rows = conv.shape
    return pl.pallas_call(
        mix_first_body,
        out_shape=shape_of((rows, weight.shape[1]), dtype),
        in_specs=[VMEM] * 3,
        out_specs=VMEM,
        compiler_params=PARAMS,
        cost_estimate=cost(2 * devices * first * rows * weight.shape[1], 8 * rows * weight.shape[1]),
        name="mix_first",
    )(conv, gate, weight)


def mix_rest_body(partial, gate, weight, *refs):
    messages, out, gathered = refs[:-2], refs[-2], refs[-1]
    devices, rest, rows = gathered.shape
    width = gate.shape[0]
    per = width // devices
    chip, core = place()
    for slot, message in enumerate(messages):
        base = 2 * jnp.bitwise_xor(chip, slot)
        gathered[base + core] = message[0]
        gathered[base + 1 - core] = message[1]
    silu = gate[...].reshape(devices, per, rows)[:, per - rest :]
    gated = (gathered[...].astype(f32) * silu).astype(bf16).reshape(devices * rest, rows)
    used = weight[...].reshape(devices, per, weight.shape[1])[:, per - rest :]
    used = used.reshape(devices * rest, weight.shape[1])
    total = partial[...] + jnp.dot(gated.T, used, preferred_element_type=f32)
    out[...] = total.astype(bf16)


def mix_rest(partial, gate, weight, messages):
    _, rest, rows = messages[0].shape
    devices = 2 * len(messages)
    return pl.pallas_call(
        mix_rest_body,
        out_shape=shape_of(partial.shape),
        in_specs=[VMEM] * (3 + len(messages)),
        out_specs=VMEM,
        scratch_shapes=[pltpu.VMEM((devices, rest, rows), bf16)],
        compiler_params=PARAMS,
        cost_estimate=cost(2 * devices * rest * rows * weight.shape[1], 8 * rows * weight.shape[1]),
        name="mix_rest",
    )(partial, gate, weight, *messages)


def to_core(block, devices):
    return lax.ppermute(block, "seq", [(i, i ^ 1) for i in range(devices)])


def to_chips(messages, devices):
    got = [messages[0]]
    for slot in range(1, len(messages)):
        got.append(lax.ppermute(messages[slot], "seq", [(i, i ^ (2 * slot)) for i in range(devices)]))
    return got


def body(tokens, value_weight, gate_weight, out_weight, kernel_weight, kernel_bias):
    rows, width = tokens.shape
    devices = lax.axis_size("seq")
    per = width // devices
    splits = per % (2 * TILE) == 0 and devices & (devices - 1) == 0
    first = per // 2 if splits else per
    blocks, *pair = project(tokens, value_weight, kernel_weight, kernel_bias, devices, first)
    columns = lax.all_to_all(blocks, "seq", split_axis=0, concat_axis=0, tiled=True)
    if splits:
        pair = [pair[0], to_core(pair[1], devices)]
    gate, *messages = gate_columns(tokens, gate_weight, pair)
    if splits:
        messages = to_chips(messages, devices)
    before = [] if splits else [gate]
    convolved, plus, minus = convolve_first(columns, first, rows, before)
    returned = lax.all_to_all(convolved, "seq", split_axis=0, concat_axis=0, tiled=True)
    if not splits:
        return mix_first(returned, gate, out_weight, bf16)
    keep, other = convolve_rest(plus, minus, messages)
    messages = to_chips(join(keep, to_core(other, devices)), devices)
    partial = mix_first(returned, gate, out_weight, f32)
    return mix_rest(partial, gate, out_weight, messages)


def solution(mesh):
    placed = (P(("grp", "seq"), None), P(), P(), P(), P(), P())
    return jax.shard_map(
        body, mesh=mesh, in_specs=placed, out_specs=P(("grp", "seq"), None), check_vma=False
    )
```

profile of v0, /device:TPU:0, one launch (start us, length us, event | category | flops | bytes accessed | tf_op | source)
XLA Modules:
  0.0 72.9 jit_solution(6314917015470156680)
XLA Ops:
  0.0 1.3 %copy.7.lag_bias = f32[16,1]{1,0:T(8,128)} copy(f32[16,1]{0,1:T(1,128)} %bitcast.2) | data formatting | bytes 128 | tf_op jit(solution)/shard_map/reshape | solution.py:99
  1.3 5.4 %project.1 = (bf16[16,144,128]{2,1,0:T(8,128)(2,1)}, bf16[8,32,512]{2,1,0:T(8,128)(2,1)}, bf16[8,32,512]{2,1,0:T(8,128)(2,1)}) custom-call(bf16[512,1024]{1,0:T(8,128)(2,1)} %tokens.3, bf16[1024,1024]{1,0:T(8,128)(2,1)} %weight.4, bf16[16,1024]{1,0:T(8,128)(2,1)} %bitcast.3, f32[16,1]{1,0:T(8,128)} %copy.7.lag_bias), custom_call_target="tpu_custom_call" | custom-call | flops 1073741824 | bytes 4194304 | tf_op jit(solution)/shard_map/project/pallas_call | solution.py:84
  6.7 7.4 %all-to-all-start = ((bf16[16,144,128]{2,1,0:T(8,128)(2,1)}), bf16[16,144,128]{2,1,0:T(8,128)(2,1)S(1)}, u32[]{:S(2)}, u32[]{:S(2)}) async-start(bf16[16,144,128]{2,1,0:T(8,128)(2,1)} %get-tuple-element.30), calls=%async_computation | async-start | bytes 1179648 | tf_op jit(solution)/shard_map/all_to_all | solution.py:360
  14.5 1.4 %collective-permute-done.refs_1_ = bf16[8,32,512]{2,1,0:T(8,128)(2,1)S(1)} collective-permute-done((bf16[8,32,512]{2,1,0:T(8,128)(2,1)}, bf16[8,32,512]{2,1,0:T(8,128)(2,1)S(1)}, u32[]{:S(2)}, u32[]{:S(2)}) %collective-permute-start) | collective-permute-done | bytes 262176 | tf_op jit(solution)/shard_map/ppermute | solution.py:343
  18.1 3.8 %gate.1 = (f32[1024,512]{1,0:T(8,128)S(1)}, bf16[2,32,512]{2,1,0:T(8,128)(2,1)S(1)}, bf16[2,32,512]{2,1,0:T(8,128)(2,1)S(1)}, bf16[2,32,512]{2,1,0:T(8,128)(2,1)...) custom-call(bf16[512,1024]{1,0:T(8,128)(2,1)S(1)} %copy-done.4, ...), custom_call_target="tpu_custom_call" | custom-call | flops 1073741824 | bytes 4194304 | tf_op jit(solution)/shard_map/gate/pallas_call | solution.py:126
  21.9 1.9 %collective-permute-start.1 = (bf16[2,32,512]{2,1,0:T(8,128)(2,1)S(1)}, bf16[2,32,512]{2,1,0:T(8,128)(2,1)S(1)}, u32[]{:S(2)}, u32[]{:S(2)}) collective-permute-start(bf16[2,32,512]{2,1,0:T(8,128)(2,1)S(1)} %get-tuple-element.38), channel_id=1, source_target_pairs={{0,2},{1,3},{2,0},{3,1},{4,6},{5,7},{6,4},{7,5},{8,10},{9,11},{10,... | collective-permute-start | bytes 196616 | tf_op jit(solution)/shard_map/ppermute | solution.py:349
  23.8 1.5 %collective-permute-start.2 = (bf16[2,32,512]{2,1,0:T(8,128)(2,1)S(1)}, bf16[2,32,512]{2,1,0:T(8,128)(2,1)S(1)}, u32[]{:S(2)}, u32[]{:S(2)}) collective-permute-start(bf16[2,32,512]{2,1,0:T(8,128)(2,1)S(1)} %get-tuple-element.39), channel_id=1, source_target_pairs={{0,4},{1,5},{2,6},{3,7},{4,0},{5,1},{6,2},{7,3},{8,12},{9,13},{10,... | collective-permute-start | bytes 196616 | tf_op jit(solution)/shard_map/ppermute | solution.py:349
  25.5 2.8 %collective-permute-start.4 = (bf16[2,32,512]{2,1,0:T(8,128)(2,1)S(1)}, bf16[2,32,512]{2,1,0:T(8,128)(2,1)S(1)}, u32[]{:S(2)}, u32[]{:S(2)}) collective-permute-start(bf16[2,32,512]{2,1,0:T(8,128)(2,1)S(1)} %get-tuple-element.41), channel_id=1, source_target_pairs={{0,8},{1,9},{2,10},{3,11},{4,12},{5,13},{6,14},{7,15},{8,0},{9,1},... | collective-permute-start | bytes 196616 | tf_op jit(solution)/shard_map/ppermute | solution.py:349
  28.2 1.5 %collective-permute-start.5 = (bf16[2,32,512]{2,1,0:T(8,128)(2,1)S(1)}, bf16[2,32,512]{2,1,0:T(8,128)(2,1)S(1)}, u32[]{:S(2)}, u32[]{:S(2)}) collective-permute-start(bf16[2,32,512]{2,1,0:T(8,128)(2,1)S(1)} %get-tuple-element.42), channel_id=1, source_target_pairs={{0,10},{1,11},{2,8},{3,9},{4,14},{5,15},{6,12},{7,13},{8,2},{9,3},... | collective-permute-start | bytes 196616 | tf_op jit(solution)/shard_map/ppermute | solution.py:349
  29.7 3.3 %collective-permute-start.6 = (bf16[2,32,512]{2,1,0:T(8,128)(2,1)S(1)}, bf16[2,32,512]{2,1,0:T(8,128)(2,1)S(1)}, u32[]{:S(2)}, u32[]{:S(2)}) collective-permute-start(bf16[2,32,512]{2,1,0:T(8,128)(2,1)S(1)} %get-tuple-element.43), channel_id=1, source_target_pairs={{0,12},{1,13},{2,14},{3,15},{4,8},{5,9},{6,10},{7,11},{8,4},{9,5},... | collective-permute-start | bytes 196616 | tf_op jit(solution)/shard_map/ppermute | solution.py:349
  33.5 3.3 %conv_first.1 = (bf16[16,32,512]{2,1,0:T(8,128)(2,1)}, bf16[128,4480]{1,0:T(8,128)(2,1)S(1)}, bf16[128,4480]{1,0:T(8,128)(2,1)S(1)}) custom-call(bf16[16,144,128]{2,1,0:T(8,128)(2,1)S(1)} %all-to-all-done.values), custom_call_target="tpu_custom_call" | custom-call | flops 1000000 | bytes 100000 | tf_op jit(solution)/shard_map/conv_first/pallas_call | solution.py:217
  38.8 5.6 %all-to-all-start.1 = ((bf16[16,32,512]{2,1,0:T(8,128)(2,1)}), bf16[16,32,512]{2,1,0:T(8,128)(2,1)S(1)}, u32[]{:S(2)}, u32[]{:S(2)}) async-start(bf16[16,32,512]{2,1,0:T(8,128)(2,1)} %get-tuple-element.31), calls=%async_computation.1 | async-start | bytes 1048576 | tf_op jit(solution)/shard_map/all_to_all | solution.py:368
  44.5 1.2 %copy-done.1 = bf16[128,4480]{1,0:T(8,128)(2,1)S(1)} copy-done((bf16[128,4480]{1,0:T(8,128)(2,1)S(1)}, bf16[128,4480]{1,0:T(8,128)(2,1)}, u32[]{:S(2)}) %copy-start.1) | copy-done | bytes 1146904
  45.7 1.3 %copy-done.3 = bf16[128,4480]{1,0:T(8,128)(2,1)S(1)} copy-done((bf16[128,4480]{1,0:T(8,128)(2,1)S(1)}, bf16[128,4480]{1,0:T(8,128)(2,1)}, u32[]{:S(2)}) %copy-start.3) | copy-done | bytes 1146904
  47.0 2.4 %conv_rest.1 = (bf16[8,32,512]{2,1,0:T(8,128)(2,1)S(1)}, bf16[8,32,512]{2,1,0:T(8,128)(2,1)S(1)}) custom-call(bf16[128,4480]{1,0:T(8,128)(2,1)S(1)} %copy-done.1, bf16[128,4480]{1,0:T(8,128)(2,1)S(1)} %copy-done.3, bf16[2,32,512]{2,1,0:T(8,128)(2,1)S(1)} %get-tuple-element.37.refs_0_, bf16[2,32,512]{2,1,0:T(8,128)(2,1)S(1)} %collective-permute-done.1.refs_1_, ...), custom_call_target="tpu_custom_call" | custom-call | flops 60000002048 | bytes 100000000 | tf_op jit(solution)/shard_map/conv_rest/pallas_call | solution.py:254
  51.1 2.0 %collective-permute-start.9 = (bf16[2,32,512]{2,1,0:T(8,128)(2,1)S(1)}, bf16[2,32,512]{2,1,0:T(8,128)(2,1)S(1)}, u32[]{:S(2)}, u32[]{:S(2)}) collective-permute-start(bf16[2,32,512]{2,1,0:T(8,128)(2,1)S(1)} %get-tuple-element.48), channel_id=1, source_target_pairs={{0,2},{1,3},{2,0},{3,1},{4,6},{5,7},{6,4},{7,5},{8,10},{9,11},{10,... | collective-permute-start | bytes 196616 | tf_op jit(solution)/shard_map/ppermute | solution.py:349
  53.0 1.5 %collective-permute-start.10 = (bf16[2,32,512]{2,1,0:T(8,128)(2,1)S(1)}, bf16[2,32,512]{2,1,0:T(8,128)(2,1)S(1)}, u32[]{:S(2)}, u32[]{:S(2)}) collective-permute-start(bf16[2,32,512]{2,1,0:T(8,128)(2,1)S(1)} %get-tuple-element.49), channel_id=1, source_target_pairs={{0,4},{1,5},{2,6},{3,7},{4,0},{5,1},{6,2},{7,3},{8,12},{9,13},{10,... | collective-permute-start | bytes 196616 | tf_op jit(solution)/shard_map/ppermute | solution.py:349
  54.6 2.8 %collective-permute-start.12 = (bf16[2,32,512]{2,1,0:T(8,128)(2,1)S(1)}, bf16[2,32,512]{2,1,0:T(8,128)(2,1)S(1)}, u32[]{:S(2)}, u32[]{:S(2)}) collective-permute-start(bf16[2,32,512]{2,1,0:T(8,128)(2,1)S(1)} %get-tuple-element.51), channel_id=1, source_target_pairs={{0,8},{1,9},{2,10},{3,11},{4,12},{5,13},{6,14},{7,15},{8,0},{9,1},... | collective-permute-start | bytes 196616 | tf_op jit(solution)/shard_map/ppermute | solution.py:349
  57.4 1.5 %collective-permute-start.13 = (bf16[2,32,512]{2,1,0:T(8,128)(2,1)S(1)}, bf16[2,32,512]{2,1,0:T(8,128)(2,1)S(1)}, u32[]{:S(2)}, u32[]{:S(2)}) collective-permute-start(bf16[2,32,512]{2,1,0:T(8,128)(2,1)S(1)} %get-tuple-element.52), channel_id=1, source_target_pairs={{0,10},{1,11},{2,8},{3,9},{4,14},{5,15},{6,12},{7,13},{8,2},{9,3},... | collective-permute-start | bytes 196616 | tf_op jit(solution)/shard_map/ppermute | solution.py:349
  58.9 3.3 %collective-permute-start.14 = (bf16[2,32,512]{2,1,0:T(8,128)(2,1)S(1)}, bf16[2,32,512]{2,1,0:T(8,128)(2,1)S(1)}, u32[]{:S(2)}, u32[]{:S(2)}) collective-permute-start(bf16[2,32,512]{2,1,0:T(8,128)(2,1)S(1)} %get-tuple-element.53), channel_id=1, source_target_pairs={{0,12},{1,13},{2,14},{3,15},{4,8},{5,9},{6,10},{7,11},{8,4},{9,5},... | collective-permute-start | bytes 196616 | tf_op jit(solution)/shard_map/ppermute | solution.py:349
  62.6 2.3 %mix_first.1.partial = f32[512,1024]{1,0:T(8,128)S(1)} custom-call(bf16[16,32,512]{2,1,0:T(8,128)(2,1)S(1)} %all-to-all-done.1.conv, f32[1024,512]{1,0:T(8,128)S(1)} %get-tuple-element.34.gate, bf16[1024,1024]{1,0:T(8,128)(2,1)} %weight.7), custom_call_target="tpu_custom_call" | custom-call | flops 536870912 | bytes 4194304 | tf_op jit(solution)/shard_map/mix_first/pallas_call | solution.py:298
  65.0 1.5 %collective-permute-done.12.refs_4_ = bf16[2,32,512]{2,1,0:T(8,128)(2,1)S(1)} collective-permute-done((bf16[2,32,512]{2,1,0:T(8,128)(2,1)S(1)}, bf16[2,32,512]{2,1,0:T(8,128)(2,1)S(1)}, u32[]{:S(2)}, u32[]{:S(2)}) %collective-permute-start.12) | collective-permute-done | bytes 65568 | tf_op jit(solution)/shard_map/ppermute | solution.py:349
  66.5 3.0 %collective-permute-done.13.refs_5_ = bf16[2,32,512]{2,1,0:T(8,128)(2,1)S(1)} collective-permute-done((bf16[2,32,512]{2,1,0:T(8,128)(2,1)S(1)}, bf16[2,32,512]{2,1,0:T(8,128)(2,1)S(1)}, u32[]{:S(2)}, u32[]{:S(2)}) %collective-permute-start.13) | collective-permute-done | bytes 65568 | tf_op jit(solution)/shard_map/ppermute | solution.py:349
  69.5 3.4 %mix_rest.1 = bf16[512,1024]{1,0:T(8,128)(2,1)} custom-call(f32[512,1024]{1,0:T(8,128)S(1)} %mix_first.1.partial, f32[1024,512]{1,0:T(8,128)S(1)} %get-tuple-element.34.gate, bf16[1024,1024]{1,0:T(8,128)(2,1)} %weight.7, bf16[2,32,512]{2,1,0:T(8,128)(2,1)S(1)} %get-tuple-element.47.refs_0_, bf16[2,32,512]{2,1,0:T(8,128)(2,1)S(1)} %collective-permute-done.9.refs_1_, ...), custom_call_target="tpu_custom_call" | custom-call | flops 536870912 | bytes 4194304 | tf_op jit(solution)/shard_map/mix_rest/pallas_call | solution.py:330
  (32 shorter events, 7.6 us)
Async XLA Ops:
  6.7 26.8 %all-to-all-start = ((bf16[16,144,128]{2,1,0:T(8,128)(2,1)}), bf16[16,144,128]{2,1,0:T(8,128)(2,1)S(1)}, u32[]{:S(2)}, u32[]{:S(2)}) async-start(bf16[16,144,128]{2,1,0:T(8,128)(2,1)} %get-tuple-element.30), calls=%async_computation | async-start | bytes 1179648 | tf_op jit(solution)/shard_map/all_to_all | solution.py:360
  14.1 1.8 %collective-permute-start = (bf16[8,32,512]{2,1,0:T(8,128)(2,1)}, bf16[8,32,512]{2,1,0:T(8,128)(2,1)S(1)}, u32[]{:S(2)}, u32[]{:S(2)}) collective-permute-start(bf16[8,32,512]{2,1,0:T(8,128)(2,1)} %get-tuple-element.33), channel_id=1, source_target_pairs={{0,1},{1,0},{2,3},{3,2},{4,5},{5,4},{6,7},{7,6},{8,9},{9,8},{10,11... | collective-permute-start | bytes 786440 | tf_op jit(solution)/shard_map/ppermute | solution.py:343
  15.9 1.2 %copy-start.4 = (bf16[512,1024]{1,0:T(8,128)(2,1)S(1)}, bf16[512,1024]{1,0:T(8,128)(2,1)}, u32[]{:S(2)}) copy-start(bf16[512,1024]{1,0:T(8,128)(2,1)} %tokens.3) | copy-start | bytes 3145732
  17.2 0.9 %copy-start.5 = (bf16[8,32,512]{2,1,0:T(8,128)(2,1)S(1)}, bf16[8,32,512]{2,1,0:T(8,128)(2,1)}, u32[]{:S(2)}) copy-start(bf16[8,32,512]{2,1,0:T(8,128)(2,1)} %get-tuple-element.32.refs_0_) | copy-start | bytes 786436
  21.9 7.8 %collective-permute-start.1 = (bf16[2,32,512]{2,1,0:T(8,128)(2,1)S(1)}, bf16[2,32,512]{2,1,0:T(8,128)(2,1)S(1)}, u32[]{:S(2)}, u32[]{:S(2)}) collective-permute-start(bf16[2,32,512]{2,1,0:T(8,128)(2,1)S(1)} %get-tuple-element.38), channel_id=1, source_target_pairs={{0,2},{1,3},{2,0},{3,1},{4,6},{5,7},{6,4},{7,5},{8,10},{9,11},{10,... | collective-permute-start | bytes 196616 | tf_op jit(solution)/shard_map/ppermute | solution.py:349
  23.8 9.1 %collective-permute-start.2 = (bf16[2,32,512]{2,1,0:T(8,128)(2,1)S(1)}, bf16[2,32,512]{2,1,0:T(8,128)(2,1)S(1)}, u32[]{:S(2)}, u32[]{:S(2)}) collective-permute-start(bf16[2,32,512]{2,1,0:T(8,128)(2,1)S(1)} %get-tuple-element.39), channel_id=1, source_target_pairs={{0,4},{1,5},{2,6},{3,7},{4,0},{5,1},{6,2},{7,3},{8,12},{9,13},{10,... | collective-permute-start | bytes 196616 | tf_op jit(solution)/shard_map/ppermute | solution.py:349
  25.3 19.1 %collective-permute-start.3 = (bf16[2,32,512]{2,1,0:T(8,128)(2,1)S(1)}, bf16[2,32,512]{2,1,0:T(8,128)(2,1)S(1)}, u32[]{:S(2)}, u32[]{:S(2)}) collective-permute-start(bf16[2,32,512]{2,1,0:T(8,128)(2,1)S(1)} %get-tuple-element.40), channel_id=1, source_target_pairs={{0,6},{1,7},{2,4},{3,5},{4,2},{5,3},{6,0},{7,1},{8,14},{9,15},{10,... | collective-permute-start | bytes 196616 | tf_op jit(solution)/shard_map/ppermute | solution.py:349
  25.5 19.0 %collective-permute-start.4 = (bf16[2,32,512]{2,1,0:T(8,128)(2,1)S(1)}, bf16[2,32,512]{2,1,0:T(8,128)(2,1)S(1)}, u32[]{:S(2)}, u32[]{:S(2)}) collective-permute-start(bf16[2,32,512]{2,1,0:T(8,128)(2,1)S(1)} %get-tuple-element.41), channel_id=1, source_target_pairs={{0,8},{1,9},{2,10},{3,11},{4,12},{5,13},{6,14},{7,15},{8,0},{9,1},... | collective-permute-start | bytes 196616 | tf_op jit(solution)/shard_map/ppermute | solution.py:349
  28.2 16.2 %collective-permute-start.5 = (bf16[2,32,512]{2,1,0:T(8,128)(2,1)S(1)}, bf16[2,32,512]{2,1,0:T(8,128)(2,1)S(1)}, u32[]{:S(2)}, u32[]{:S(2)}) collective-permute-start(bf16[2,32,512]{2,1,0:T(8,128)(2,1)S(1)} %get-tuple-element.42), channel_id=1, source_target_pairs={{0,10},{1,11},{2,8},{3,9},{4,14},{5,15},{6,12},{7,13},{8,2},{9,3},... | collective-permute-start | bytes 196616 | tf_op jit(solution)/shard_map/ppermute | solution.py:349
  29.7 14.8 %collective-permute-start.6 = (bf16[2,32,512]{2,1,0:T(8,128)(2,1)S(1)}, bf16[2,32,512]{2,1,0:T(8,128)(2,1)S(1)}, u32[]{:S(2)}, u32[]{:S(2)}) collective-permute-start(bf16[2,32,512]{2,1,0:T(8,128)(2,1)S(1)} %get-tuple-element.43), channel_id=1, source_target_pairs={{0,12},{1,13},{2,14},{3,15},{4,8},{5,9},{6,10},{7,11},{8,4},{9,5},... | collective-permute-start | bytes 196616 | tf_op jit(solution)/shard_map/ppermute | solution.py:349
  33.0 11.5 %collective-permute-start.7 = (bf16[2,32,512]{2,1,0:T(8,128)(2,1)S(1)}, bf16[2,32,512]{2,1,0:T(8,128)(2,1)S(1)}, u32[]{:S(2)}, u32[]{:S(2)}) collective-permute-start(bf16[2,32,512]{2,1,0:T(8,128)(2,1)S(1)} %get-tuple-element.44), channel_id=1, source_target_pairs={{0,14},{1,15},{2,12},{3,13},{4,10},{5,11},{6,8},{7,9},{8,6},{9,7},... | collective-permute-start | bytes 196616 | tf_op jit(solution)/shard_map/ppermute | solution.py:349
  36.8 1.0 %copy-start = (bf16[128,4480]{1,0:T(8,128)(2,1)}, bf16[128,4480]{1,0:T(8,128)(2,1)S(1)}, u32[]{:S(2)}) copy-start(bf16[128,4480]{1,0:T(8,128)(2,1)S(1)} %get-tuple-element.35.plus) | copy-start | bytes 3440644
  37.8 1.0 %copy-start.2 = (bf16[128,4480]{1,0:T(8,128)(2,1)}, bf16[128,4480]{1,0:T(8,128)(2,1)S(1)}, u32[]{:S(2)}) copy-start(bf16[128,4480]{1,0:T(8,128)(2,1)S(1)} %get-tuple-element.36.minus) | copy-start | bytes 3440644
  38.8 23.8 %all-to-all-start.1 = ((bf16[16,32,512]{2,1,0:T(8,128)(2,1)}), bf16[16,32,512]{2,1,0:T(8,128)(2,1)S(1)}, u32[]{:S(2)}, u32[]{:S(2)}) async-start(bf16[16,32,512]{2,1,0:T(8,128)(2,1)} %get-tuple-element.31), calls=%async_computation.1 | async-start | bytes 1048576 | tf_op jit(solution)/shard_map/all_to_all | solution.py:368
  44.5 1.3 %copy-start.1 = (bf16[128,4480]{1,0:T(8,128)(2,1)S(1)}, bf16[128,4480]{1,0:T(8,128)(2,1)}, u32[]{:S(2)}) copy-start(bf16[128,4480]{1,0:T(8,128)(2,1)} %copy-done) | copy-start | bytes 3440644
  45.7 1.3 %copy-start.3 = (bf16[128,4480]{1,0:T(8,128)(2,1)S(1)}, bf16[128,4480]{1,0:T(8,128)(2,1)}, u32[]{:S(2)}) copy-start(bf16[128,4480]{1,0:T(8,128)(2,1)} %copy-done.2) | copy-start | bytes 3440644
  49.4 1.6 %collective-permute-start.8 = (bf16[8,32,512]{2,1,0:T(8,128)(2,1)S(1)}, bf16[8,32,512]{2,1,0:T(8,128)(2,1)S(1)}, u32[]{:S(2)}, u32[]{:S(2)}) collective-permute-start(bf16[8,32,512]{2,1,0:T(8,128)(2,1)S(1)} %get-tuple-element.46), channel_id=1, source_target_pairs={{0,1},{1,0},{2,3},{3,2},{4,5},{5,4},{6,7},{7,6},{8,9},{9,8},{10,11... | collective-permute-start | bytes 786440 | tf_op jit(solution)/shard_map/ppermute | solution.py:343
  51.1 7.8 %collective-permute-start.9 = (bf16[2,32,512]{2,1,0:T(8,128)(2,1)S(1)}, bf16[2,32,512]{2,1,0:T(8,128)(2,1)S(1)}, u32[]{:S(2)}, u32[]{:S(2)}) collective-permute-start(bf16[2,32,512]{2,1,0:T(8,128)(2,1)S(1)} %get-tuple-element.48), channel_id=1, source_target_pairs={{0,2},{1,3},{2,0},{3,1},{4,6},{5,7},{6,4},{7,5},{8,10},{9,11},{10,... | collective-permute-start | bytes 196616 | tf_op jit(solution)/shard_map/ppermute | solution.py:349
  53.0 9.1 %collective-permute-start.10 = (bf16[2,32,512]{2,1,0:T(8,128)(2,1)S(1)}, bf16[2,32,512]{2,1,0:T(8,128)(2,1)S(1)}, u32[]{:S(2)}, u32[]{:S(2)}) collective-permute-start(bf16[2,32,512]{2,1,0:T(8,128)(2,1)S(1)} %get-tuple-element.49), channel_id=1, source_target_pairs={{0,4},{1,5},{2,6},{3,7},{4,0},{5,1},{6,2},{7,3},{8,12},{9,13},{10,... | collective-permute-start | bytes 196616 | tf_op jit(solution)/shard_map/ppermute | solution.py:349
  54.5 10.5 %collective-permute-start.11 = (bf16[2,32,512]{2,1,0:T(8,128)(2,1)S(1)}, bf16[2,32,512]{2,1,0:T(8,128)(2,1)S(1)}, u32[]{:S(2)}, u32[]{:S(2)}) collective-permute-start(bf16[2,32,512]{2,1,0:T(8,128)(2,1)S(1)} %get-tuple-element.50), channel_id=1, source_target_pairs={{0,6},{1,7},{2,4},{3,5},{4,2},{5,3},{6,0},{7,1},{8,14},{9,15},{10,... | collective-permute-start | bytes 196616 | tf_op jit(solution)/shard_map/ppermute | solution.py:349
  54.6 11.9 %collective-permute-start.12 = (bf16[2,32,512]{2,1,0:T(8,128)(2,1)S(1)}, bf16[2,32,512]{2,1,0:T(8,128)(2,1)S(1)}, u32[]{:S(2)}, u32[]{:S(2)}) collective-permute-start(bf16[2,32,512]{2,1,0:T(8,128)(2,1)S(1)} %get-tuple-element.51), channel_id=1, source_target_pairs={{0,8},{1,9},{2,10},{3,11},{4,12},{5,13},{6,14},{7,15},{8,0},{9,1},... | collective-permute-start | bytes 196616 | tf_op jit(solution)/shard_map/ppermute | solution.py:349
  57.4 12.1 %collective-permute-start.13 = (bf16[2,32,512]{2,1,0:T(8,128)(2,1)S(1)}, bf16[2,32,512]{2,1,0:T(8,128)(2,1)S(1)}, u32[]{:S(2)}, u32[]{:S(2)}) collective-permute-start(bf16[2,32,512]{2,1,0:T(8,128)(2,1)S(1)} %get-tuple-element.52), channel_id=1, source_target_pairs={{0,10},{1,11},{2,8},{3,9},{4,14},{5,15},{6,12},{7,13},{8,2},{9,3},... | collective-permute-start | bytes 196616 | tf_op jit(solution)/shard_map/ppermute | solution.py:349
  58.9 10.6 %collective-permute-start.14 = (bf16[2,32,512]{2,1,0:T(8,128)(2,1)S(1)}, bf16[2,32,512]{2,1,0:T(8,128)(2,1)S(1)}, u32[]{:S(2)}, u32[]{:S(2)}) collective-permute-start(bf16[2,32,512]{2,1,0:T(8,128)(2,1)S(1)} %get-tuple-element.53), channel_id=1, source_target_pairs={{0,12},{1,13},{2,14},{3,15},{4,8},{5,9},{6,10},{7,11},{8,4},{9,5},... | collective-permute-start | bytes 196616 | tf_op jit(solution)/shard_map/ppermute | solution.py:349
  62.2 7.4 %collective-permute-start.15 = (bf16[2,32,512]{2,1,0:T(8,128)(2,1)S(1)}, bf16[2,32,512]{2,1,0:T(8,128)(2,1)S(1)}, u32[]{:S(2)}, u32[]{:S(2)}) collective-permute-start(bf16[2,32,512]{2,1,0:T(8,128)(2,1)S(1)} %get-tuple-element.54), channel_id=1, source_target_pairs={{0,14},{1,15},{2,12},{3,13},{4,10},{5,11},{6,8},{7,9},{8,6},{9,7},... | collective-permute-start | bytes 196616 | tf_op jit(solution)/shard_map/ppermute | solution.py:349
where the time goes:
time: 73.5 us; the launch traced here: 72.9 us
  starting transfers between devices  37 us (50%)
  Pallas kernels  20.6 us (28%)
  local copies, waits for them, and re-layouts  8.04 us (11%)
  waiting for transfers between devices  7.13 us (10%)
    ppermute x14, starting transfers between devices, to_chips(): lax.ppermute(messages[slot], 'seq', [(i, i ^ 2 * slot) for i in range(dev...  23.1 us
    all_to_all x1, starting transfers between devices, body(): lax.all_to_all(blocks, 'seq', split_axis=0, concat_axis=0, tiled=True)  7.39 us
    unnamed x12, local copies, waits for them, and re-layouts  6.72 us
    all_to_all x1, starting transfers between devices, body(): lax.all_to_all(convolved, 'seq', split_axis=0, concat_axis=0, tiled=True)  5.58 us
    pallas_call x1, Pallas kernels, project(): pl.pallas_call(functools.partial(project_body, (devices, per, first, head...  5.4 us
    ppermute x14, waiting for transfers between devices, to_chips(): lax.ppermute(messages[slot], 'seq', [(i, i ^ 2 * slot) for i in range(dev...  4.57 us
    pallas_call x1, Pallas kernels, gate_columns(): pl.pallas_call(gate_body, grid=(width // step,), out_shape=outs, in_specs...  3.78 us
    pallas_call x1, Pallas kernels, mix_rest(): pl.pallas_call(mix_rest_body, out_shape=shape_of(partial.shape), in_specs...  3.36 us
  transfers between devices with their start and end apart: 18, of which 4 were waited for; matrix products, arithmetic and copies ran while one was open for 0% of the time, Pallas kernels for 16%

commit v1 on v0

v1 whole, which is shorter than its diff:
```python
import functools

import jax
import jax.numpy as jnp
from jax import lax
from jax.experimental import pallas as pl
from jax.experimental.pallas import tpu as pltpu
from jax.sharding import PartitionSpec as P

f32 = jnp.float32
bf16 = jnp.bfloat16
LANES = 128
TILE = 16
VMEM = pl.BlockSpec(memory_space=pltpu.VMEM)
HBM = pl.BlockSpec(memory_space=pltpu.HBM)
PARAMS = pltpu.CompilerParams(vmem_limit_bytes=48 * 2**20)
SMALL = pltpu.CompilerParams(vmem_limit_bytes=24 * 2**20)
LARGE = pltpu.CompilerParams(vmem_limit_bytes=62 * 2**20)


def cost(flops, nbytes):
    return pl.CostEstimate(flops=int(flops), bytes_accessed=int(nbytes), transcendentals=0)


def whole_block(shape):
    return pl.BlockSpec(shape, lambda i: (0,) * len(shape))


def shape_of(shape, dtype=bf16):
    return jax.ShapeDtypeStruct(shape, dtype)


def place():
    me = lax.axis_index("seq")
    return me // 2, lax.rem(me, 2)


def project_body(sizes, tokens, weight, lag_weight, lag_bias, *refs):
    devices, per, first, heads, pieces = sizes
    out, messages = refs[0], refs[1:-8]
    tokens_here, weight_here, out_here, rest_here, token_done, weight_done, out_done, rest_done = refs[-8:]
    rows, width = tokens.shape
    tiles = rows // LANES
    step = width // pieces
    count = step // per
    reading, writing = [], []
    for at in range(pieces):
        cut = (slice(None), slice(step * at, step * at + step))
        reading.append(pltpu.make_async_copy(weight.at[cut], weight_here.at[cut], weight_done.at[at]))
        cut = slice(count * at, count * at + count)
        writing.append(pltpu.make_async_copy(out_here.at[cut], out.at[cut], out_done.at[at]))
    token_copy = pltpu.make_async_copy(tokens, tokens_here, token_done.at[0])
    token_copy.start()
    reading[0].start()
    square = (heads, heads)
    on_line = lax.broadcasted_iota(jnp.int32, square, 0) == lax.broadcasted_iota(jnp.int32, square, 1)
    bias = jnp.sum(jnp.where(on_line, jnp.broadcast_to(lag_bias[...], square), 0.0), axis=1, keepdims=True)
    lag_columns = lag_weight[...].T
    token_copy.wait()
    for copy in reading[1:]:
        copy.start()
    logits = jnp.dot(tokens_here[...], lag_columns, preferred_element_type=f32).T + bias
    lag_rows = jnp.tanh(logits) * (rows * devices) ** (-0.5)
    chip, _ = place()
    for at in range(pieces):
        reading[at].wait()
        part = jnp.dot(
            tokens_here[...], weight_here[:, step * at : step * at + step], preferred_element_type=f32
        )
        part = part.astype(bf16).T
        for group in range(count):
            device = at * count + group
            block = part[per * group : per * group + first]
            for tile in range(tiles):
                out_here[device, first * tile : first * tile + first] = block[
                    :, LANES * tile : LANES * tile + LANES
                ]
            head = device * heads // devices
            row = lag_rows[head : head + 1]
            lines = [row[:, LANES * tile : LANES * tile + LANES] for tile in range(tiles)]
            lines.append(jnp.zeros((out.shape[1] - first * tiles - tiles, LANES), f32))
            out_here[device, first * tiles :] = jnp.concatenate(lines, axis=0).astype(bf16)
        writing[at].start()
        if first < per:
            for group in range(count):
                device = at * count + group
                slot = jnp.bitwise_xor(chip, device // 2)
                rest_here[slot, device % 2] = part[per * group + first : per * group + per]
    for slot, message in enumerate(messages):
        writing.append(pltpu.make_async_copy(rest_here.at[slot], message, rest_done.at[slot]))
        writing[-1].start()
    for copy in writing:
        copy.wait()


def project(tokens, weight, lag_weight, lag_bias, devices, first):
    rows, width = tokens.shape
    heads = lag_weight.shape[1]
    per = width // devices
    pieces = max(1, min(2, devices // 2))
    tall = first * (rows // LANES) + TILE
    outs = [shape_of((devices, tall, LANES))]
    if first < per:
        outs += [shape_of((2, per - first, rows))] * (devices // 2)
    return pl.pallas_call(
        functools.partial(project_body, (devices, per, first, heads, pieces)),
        out_shape=outs,
        in_specs=[HBM, HBM, VMEM, VMEM],
        out_specs=[HBM] * len(outs),
        scratch_shapes=[
            pltpu.VMEM((rows, width), bf16),
            pltpu.VMEM((width, width), bf16),
            pltpu.VMEM((devices, tall, LANES), bf16),
            pltpu.VMEM((devices // 2, 2, max(per - first, TILE), rows), bf16),
            pltpu.SemaphoreType.DMA((1,)),
            pltpu.SemaphoreType.DMA((pieces,)),
            pltpu.SemaphoreType.DMA((pieces,)),
            pltpu.SemaphoreType.DMA((devices // 2,)),
        ],
        compiler_params=LARGE,
        cost_estimate=cost(2 * rows * width * width, 4 * rows * width + 2 * width * width),
        name="project",
    )(tokens, weight, lag_weight.T, lag_bias.reshape(1, heads))


def fill_strips(row, plus, minus):
    length = row.shape[1]
    half = length // 2
    lead = plus.shape[1] - half
    low, high = row[:, :half] * 0.5, row[:, half:] * 0.5
    for ref, line, sign in ((plus, low + high, 1.0), (minus, low - high, -1.0)):
        for piece in range(LANES // TILE):
            turned = pltpu.roll(
                jnp.broadcast_to(line, (TILE, half)), TILE * piece, 1, stride=1, stride_axis=0
            )
            here = slice(TILE * piece, TILE * piece + TILE)
            edge = turned[:, :LANES]
            if sign < 0:
                down = lax.broadcasted_iota(jnp.int32, (TILE, LANES), 0) + TILE * piece
                across = lax.broadcasted_iota(jnp.int32, (TILE, LANES), 1)
                edge = jnp.where(across < down, -edge, edge)
            ref[here, :lead] = (turned[:, half - lead :] * sign).astype(bf16)
            ref[here, lead : lead + LANES] = edge.astype(bf16)
            ref[here, lead + LANES :] = turned[:, LANES:].astype(bf16)


def convolve(block_of, plus, minus, twice_plus, twice_minus, acc_plus, acc_minus):
    count, channels, span = twice_plus.shape
    half = count // 2
    lead = plus.shape[1] - half * span
    for at in range(half):
        low, high = block_of(at).astype(f32), block_of(at + half).astype(f32)
        total, gap = (low + high).astype(bf16), (low - high).astype(bf16)
        twice_plus[at] = total
        twice_plus[at + half] = total
        twice_minus[at] = -gap
        twice_minus[at + half] = gap
    group = min(half, 4)
    for acc, twice, strip in ((acc_plus, twice_plus, plus), (acc_minus, twice_minus, minus)):
        for start in range(0, half, group):
            left, right = [], []
            for lag in range(start, start + group):
                left.append(twice[half - lag : 2 * half - lag].reshape(half * channels, span))
                for part in range(span // LANES):
                    begin = span * lag + lead - LANES * part
                    right.append(strip[:, begin : begin + span])
            piece = jnp.dot(
                jnp.concatenate(left, axis=1), jnp.concatenate(right, axis=0), preferred_element_type=f32
            )
            acc[...] = piece if start == 0 else acc[...] + piece


def first_body(channels, values, *refs):
    out, lag_row, plus, minus, *scratch = refs
    count, tall, _ = values.shape
    span = out.shape[2]
    tiles = span // LANES
    pieces = []
    for at in range(count):
        rows = values[at, channels * tiles :].astype(f32)
        pieces += [rows[tile : tile + 1] for tile in range(tiles)]
    lag_row[...] = jnp.concatenate(pieces, axis=1)
    fill_strips(lag_row[...], plus, minus)

    def block_of(at):
        return jnp.concatenate(
            [values[at, channels * tile : channels * tile + channels] for tile in range(tiles)], axis=1
        )

    convolve(block_of, plus, minus, *scratch)
    acc_plus, acc_minus = scratch[2:]
    half = count // 2
    out[:half] = (acc_plus[...] + acc_minus[...]).reshape(half, channels, span).astype(bf16)
    out[half:] = (acc_plus[...] - acc_minus[...]).reshape(half, channels, span).astype(bf16)


def scratch_for(count, channels, span):
    return [pltpu.VMEM((LANES, count // 2 * span + span - LANES), bf16)] * 2 + [
        pltpu.VMEM((count, channels, span), bf16)
    ] * 2 + [
        pltpu.VMEM((count // 2 * channels, span), f32)
    ] * 2


def convolve_first(values, channels, span):
    count = values.shape[0]
    return pl.pallas_call(
        functools.partial(first_body, channels),
        out_shape=[shape_of((count, channels, span)), shape_of((1, count * span), f32)],
        in_specs=[VMEM],
        out_specs=[VMEM] * 2,
        scratch_shapes=scratch_for(count, channels, span),
        compiler_params=SMALL,
        cost_estimate=cost(1e6, 1e5),
        name="conv_first",
    )(values)


def pack_body(chips, *refs):
    messages, out, done = refs[:chips], refs[-2], refs[-1]
    core = 1 - place()[1]
    copies = [
        pltpu.make_async_copy(messages[slot].at[core], out.at[slot], done.at[slot]) for slot in range(chips)
    ]
    for copy in copies:
        copy.start()
    for copy in copies:
        copy.wait()


def pack(messages, after):
    chips = len(messages)
    return pl.pallas_call(
        functools.partial(pack_body, chips),
        out_shape=shape_of((chips,) + messages[0].shape[1:]),
        in_specs=[HBM] * (chips + 1),
        out_specs=VMEM,
        scratch_shapes=[pltpu.SemaphoreType.DMA((chips,))],
        compiler_params=SMALL,
        cost_estimate=cost(6e10, 1e8),
        name="pack",
    )(*messages, after)


def rest_body(lag_row, crossed, *refs):
    chips = len(refs) - 10
    messages, keep, other = refs[:chips], refs[chips], refs[chips + 1]
    gathered, done, *scratch = refs[chips + 2 :]
    plus, minus = scratch[:2]
    chip, core = place()
    copies = []
    for slot, message in enumerate(messages):
        base = 2 * jnp.bitwise_xor(chip, slot)
        copies.append(pltpu.make_async_copy(message.at[core], gathered.at[base + core], done.at[slot]))
        copies[-1].start()
    fill_strips(lag_row[...], plus, minus)
    for slot in range(chips):
        gathered[2 * jnp.bitwise_xor(chip, slot) + 1 - core] = crossed[slot]
    for copy in copies:
        copy.wait()
    convolve(lambda at: gathered[at], *scratch)
    acc_plus, acc_minus = scratch[4:]
    count, channels, span = gathered.shape
    half = count // 2
    gathered[:half] = (acc_plus[...] + acc_minus[...]).reshape(half, channels, span).astype(bf16)
    gathered[half:] = (acc_plus[...] - acc_minus[...]).reshape(half, channels, span).astype(bf16)
    for slot in range(chips):
        base = 2 * jnp.bitwise_xor(chip, slot)
        keep[slot] = gathered[base + core]
        other[slot] = gathered[base + 1 - core]


def convolve_rest(lag_row, crossed, messages):
    chips = len(messages)
    _, channels, span = messages[0].shape
    result = shape_of((chips, channels, span))
    return pl.pallas_call(
        rest_body,
        out_shape=[result] * 2,
        in_specs=[VMEM] * 2 + [HBM] * chips,
        out_specs=[VMEM] * 2,
        scratch_shapes=[pltpu.VMEM((2 * chips, channels, span), bf16), pltpu.SemaphoreType.DMA((chips,))]
        + scratch_for(2 * chips, channels, span),
        compiler_params=SMALL,
        cost_estimate=cost(1e6, 1e5),
        name="conv_rest",
    )(lag_row, crossed, *messages)


def join_body(keep, other, *messages):
    for slot, message in enumerate(messages):
        message[0] = keep[slot]
        message[1] = other[slot]


def join(keep, other):
    chips, channels, span = keep.shape
    return pl.pallas_call(
        join_body,
        out_shape=[shape_of((2, channels, span))] * chips,
        in_specs=[VMEM] * 2,
        out_specs=[VMEM] * chips,
        compiler_params=SMALL,
        name="join",
    )(keep, other)


def mix_first_body(tokens, gate_weight, conv, weight, out, *late):
    devices, first, rows = conv.shape
    width, columns = weight.shape
    per = width // devices
    gate = jnp.dot(tokens[...], gate_weight[...], preferred_element_type=f32)
    silu = (gate / (1.0 + jnp.exp(-gate))).T.reshape(devices, per, rows)
    used = weight[...].reshape(devices, per, columns)
    gated = (conv[...].astype(f32) * silu[:, :first]).astype(bf16).reshape(devices * first, rows)
    mixed = jnp.dot(
        gated.T, used[:, :first].reshape(devices * first, columns), preferred_element_type=f32
    )
    out[...] = mixed.astype(out.dtype)
    if late:
        late[0][...] = silu[:, first:]
        late[1][...] = used[:, first:]


def mix_first(tokens, gate_weight, conv, weight):
    devices, first, rows = conv.shape
    width, columns = weight.shape
    rest = width // devices - first
    outs = [shape_of((rows, columns), f32 if rest else bf16)]
    if rest:
        outs += [shape_of((devices, rest, rows), f32), shape_of((devices, rest, columns))]
    return pl.pallas_call(
        mix_first_body,
        out_shape=outs,
        in_specs=[VMEM] * 4,
        out_specs=[VMEM] * len(outs),
        compiler_params=SMALL,
        cost_estimate=cost(4 * width * rows * columns, 8 * rows * columns),
        name="mix_first",
    )(tokens, gate_weight, conv, weight)


def mix_rest_body(partial, silu, weight, *refs):
    messages, out, gathered = refs[:-2], refs[-2], refs[-1]
    devices, rest, rows = gathered.shape
    chip, core = place()
    for slot, message in enumerate(messages):
        base = 2 * jnp.bitwise_xor(chip, slot)
        gathered[base + core] = message[0]
        gathered[base + 1 - core] = message[1]
    gated = (gathered[...].astype(f32) * silu[...]).astype(bf16).reshape(devices * rest, rows)
    used = weight[...].reshape(devices * rest, weight.shape[2])
    total = partial[...] + jnp.dot(gated.T, used, preferred_element_type=f32)
    out[...] = total.astype(bf16)


def mix_rest(partial, silu, weight, messages):
    devices, rest, rows = silu.shape
    return pl.pallas_call(
        mix_rest_body,
        out_shape=shape_of(partial.shape),
        in_specs=[VMEM] * (3 + len(messages)),
        out_specs=VMEM,
        scratch_shapes=[pltpu.VMEM((devices, rest, rows), bf16)],
        compiler_params=SMALL,
        cost_estimate=cost(2 * devices * rest * rows * weight.shape[2], 8 * rows * weight.shape[2]),
        name="mix_rest",
    )(partial, silu, weight, *messages)


def to_core(block, devices):
    return lax.ppermute(block, "seq", [(i, i ^ 1) for i in range(devices)])


def to_chips(messages, devices):
    got = [messages[0]]
    for slot in range(1, len(messages)):
        got.append(lax.ppermute(messages[slot], "seq", [(i, i ^ (2 * slot)) for i in range(devices)]))
    return got


def body(tokens, value_weight, gate_weight, out_weight, kernel_weight, kernel_bias):
    rows, width = tokens.shape
    devices = lax.axis_size("seq")
    per = width // devices
    splits = per % (2 * TILE) == 0 and devices & (devices - 1) == 0
    first = per // 2 if splits else per
    blocks, *rest = project(tokens, value_weight, kernel_weight, kernel_bias, devices, first)
    columns = lax.all_to_all(blocks, "seq", split_axis=0, concat_axis=0, tiled=True)
    if splits:
        messages = to_chips(rest, devices)
    convolved, lag_row = convolve_first(columns, first, rows)
    returned = lax.all_to_all(convolved, "seq", split_axis=0, concat_axis=0, tiled=True)
    if not splits:
        return mix_first(tokens, gate_weight, returned, out_weight)[0]
    crossed = to_core(pack(messages, lag_row), devices)
    keep, other = convolve_rest(lag_row, crossed, messages)
    messages = to_chips(join(keep, to_core(other, devices)), devices)
    return mix_rest(*mix_first(tokens, gate_weight, returned, out_weight), messages)


def solution(mesh):
    placed = (P(("grp", "seq"), None), P(), P(), P(), P(), P())
    return jax.shard_map(
        body, mesh=mesh, in_specs=placed, out_specs=P(("grp", "seq"), None), check_vma=False
    )
```

time: 73.5 us -> 69.6 us (0.947)
  starting transfers between devices: 37 us -> 44.6 us
  local copies, waits for them, and re-layouts: 8.04 us -> 2.83 us
  Pallas kernels: 20.6 us -> 16.3 us
  waiting for transfers between devices: 7.13 us -> 5.24 us
    ppermute x14, starting transfers between devices: 23.1 us -> 27.2 us  [to_chips(): lax.ppermute(messages[slot], 'seq', [(i, i ^ 2 * slot) for i in range(dev...]
    unnamed x12 -> x8, local copies, waits for them, and re-layouts: 6.72 us -> 2.83 us
    all_to_all x1, starting transfers between devices: 5.58 us -> 9.02 us  [body(): lax.all_to_all(convolved, 'seq', split_axis=0, concat_axis=0, tiled=True)]
    pallas_call x3, Pallas kernels: 8.51 us -> 6.07 us  [the longest x1 3.42 us: convolve_rest(): pl.pallas_call(rest_body, out_shape=[result] * 2, in_specs=[VMEM] * 2 + [...]
    ppermute x14, waiting for transfers between devices: 4.57 us -> 2.91 us  [to_chips(): lax.ppermute(messages[slot], 'seq', [(i, i ^ 2 * slot) for i in range(dev...]
    pallas_call x1, Pallas kernels: 3.36 us -> 1.77 us  [mix_rest(): pl.pallas_call(mix_rest_body, out_shape=shape_of(partial.shape), in_specs...]
    reshape x1 -> x0, local copies, waits for them, and re-layouts: 1.32 us -> none  [project(): lag_bias.reshape(heads, 1)]
  transfers between devices with their start and end apart: 18 -> 18, of which waited for: 4 -> 6; matrix products, arithmetic and copies ran while one was open for 0% -> 0% of each run, Pallas kernels for 16% -> 14%
where the time goes in v1:
time: 69.6 us; the launch traced here: 69.1 us
  starting transfers between devices  44.6 us (64%)
  Pallas kernels  16.3 us (23%)
  waiting for transfers between devices  5.24 us (8%)
  local copies, waits for them, and re-layouts  2.83 us (4%)
    ppermute x14, starting transfers between devices, to_chips(): lax.ppermute(messages[slot], 'seq', [(i, i ^ 2 * slot) for i in range(dev...  27.2 us
    all_to_all x1, starting transfers between devices, body(): lax.all_to_all(convolved, 'seq', split_axis=0, concat_axis=0, tiled=True)  9.02 us
    all_to_all x1, starting transfers between devices, body(): lax.all_to_all(blocks, 'seq', split_axis=0, concat_axis=0, tiled=True)  7.53 us
    pallas_call x1, Pallas kernels, project(): pl.pallas_call(functools.partial(project_body, (devices, per, first, head...  5.07 us
    pallas_call x1, Pallas kernels, convolve_rest(): pl.pallas_call(rest_body, out_shape=[result] * 2, in_specs=[VMEM] * 2 + [...  3.42 us
    pallas_call x1, Pallas kernels, convolve_first(): pl.pallas_call(functools.partial(first_body, channels), out_shape=[shape_...  3.32 us
    ppermute x14, waiting for transfers between devices, to_chips(): lax.ppermute(messages[slot], 'seq', [(i, i ^ 2 * slot) for i in range(dev...  2.91 us
    unnamed x8, local copies, waits for them, and re-layouts  2.83 us
  transfers between devices with their start and end apart: 18, of which 6 were waited for; matrix products, arithmetic and copies ran while one was open for 0% of the time, Pallas kernels for 14%

profile of v1, /device:TPU:0, one launch (start us, length us, event | category | flops | bytes accessed | tf_op | source)
XLA Modules:
  0.0 69.1 jit_solution(17283974184565822128)
XLA Ops:
  0.0 5.1 %project.1 = (bf16[16,144,128]{2,1,0:T(8,128)(2,1)}, bf16[2,32,512]{2,1,0:T(8,128)(2,1)}, bf16[2,32,512]{2,1,0:T(8,128)(2,1)}, bf16[2,32,512]{2,1,0:T(8,128)(2,1...) custom-call(bf16[512,1024]{1,0:T(8,128)(2,1)} %tokens.3, ...), custom_call_target="tpu_custom_call" | custom-call | flops 1073741824 | bytes 4194304 | tf_op jit(solution)/shard_map/project/pallas_call | solution.py:105
  5.1 7.5 %all-to-all-start = ((bf16[16,144,128]{2,1,0:T(8,128)(2,1)}), bf16[16,144,128]{2,1,0:T(8,128)(2,1)S(1)}, u32[]{:S(2)}, u32[]{:S(2)}) async-start(bf16[16,144,128]{2,1,0:T(8,128)(2,1)} %get-tuple-element.29), calls=%async_computation | async-start | bytes 1179648 | tf_op jit(solution)/shard_map/all_to_all | solution.py:389
  12.6 1.9 %collective-permute-start = (bf16[2,32,512]{2,1,0:T(8,128)(2,1)}, bf16[2,32,512]{2,1,0:T(8,128)(2,1)S(1)}, u32[]{:S(2)}, u32[]{:S(2)}) collective-permute-start(bf16[2,32,512]{2,1,0:T(8,128)(2,1)} %get-tuple-element.36), channel_id=1, source_target_pairs={{0,2},{1,3},{2,0},{3,1},{4,6},{5,7},{6,4},{7,5},{8,10},{9,11},{10,... | collective-permute-start | bytes 196616 | tf_op jit(solution)/shard_map/ppermute | solution.py:378
  14.5 1.5 %collective-permute-start.1 = (bf16[2,32,512]{2,1,0:T(8,128)(2,1)}, bf16[2,32,512]{2,1,0:T(8,128)(2,1)S(1)}, u32[]{:S(2)}, u32[]{:S(2)}) collective-permute-start(bf16[2,32,512]{2,1,0:T(8,128)(2,1)} %get-tuple-element.37), channel_id=1, source_target_pairs={{0,4},{1,5},{2,6},{3,7},{4,0},{5,1},{6,2},{7,3},{8,12},{9,13},{10,... | collective-permute-start | bytes 196616 | tf_op jit(solution)/shard_map/ppermute | solution.py:378
  16.2 2.8 %collective-permute-start.3 = (bf16[2,32,512]{2,1,0:T(8,128)(2,1)}, bf16[2,32,512]{2,1,0:T(8,128)(2,1)S(1)}, u32[]{:S(2)}, u32[]{:S(2)}) collective-permute-start(bf16[2,32,512]{2,1,0:T(8,128)(2,1)} %get-tuple-element.39), channel_id=1, source_target_pairs={{0,8},{1,9},{2,10},{3,11},{4,12},{5,13},{6,14},{7,15},{8,0},{9,1},... | collective-permute-start | bytes 196616 | tf_op jit(solution)/shard_map/ppermute | solution.py:378
  18.9 1.5 %collective-permute-start.4 = (bf16[2,32,512]{2,1,0:T(8,128)(2,1)}, bf16[2,32,512]{2,1,0:T(8,128)(2,1)S(1)}, u32[]{:S(2)}, u32[]{:S(2)}) collective-permute-start(bf16[2,32,512]{2,1,0:T(8,128)(2,1)} %get-tuple-element.40), channel_id=1, source_target_pairs={{0,10},{1,11},{2,8},{3,9},{4,14},{5,15},{6,12},{7,13},{8,2},{9,3},... | collective-permute-start | bytes 196616 | tf_op jit(solution)/shard_map/ppermute | solution.py:378
  20.6 4.2 %collective-permute-start.5 = (bf16[2,32,512]{2,1,0:T(8,128)(2,1)}, bf16[2,32,512]{2,1,0:T(8,128)(2,1)S(1)}, u32[]{:S(2)}, u32[]{:S(2)}) collective-permute-start(bf16[2,32,512]{2,1,0:T(8,128)(2,1)} %get-tuple-element.41), channel_id=1, source_target_pairs={{0,12},{1,13},{2,14},{3,15},{4,8},{5,9},{6,10},{7,11},{8,4},{9,5},... | collective-permute-start | bytes 196616 | tf_op jit(solution)/shard_map/ppermute | solution.py:378
  25.6 4.0 %collective-permute-start.6 = (bf16[2,32,512]{2,1,0:T(8,128)(2,1)}, bf16[2,32,512]{2,1,0:T(8,128)(2,1)S(1)}, u32[]{:S(2)}, u32[]{:S(2)}) collective-permute-start(bf16[2,32,512]{2,1,0:T(8,128)(2,1)} %get-tuple-element.42), channel_id=1, source_target_pairs={{0,14},{1,15},{2,12},{3,13},{4,10},{5,11},{6,8},{7,9},{8,6},{9,7},... | collective-permute-start | bytes 196616 | tf_op jit(solution)/shard_map/ppermute | solution.py:378
  29.6 3.3 %conv_first.1 = (bf16[16,32,512]{2,1,0:T(8,128)(2,1)}, f32[1,8192]{1,0:T(1,128)S(1)}) custom-call(bf16[16,144,128]{2,1,0:T(8,128)(2,1)S(1)} %all-to-all-done.values), custom_call_target="tpu_custom_call" | custom-call | flops 1000000 | bytes 100000 | tf_op jit(solution)/shard_map/conv_first/pallas_call | solution.py:207
  32.9 9.0 %all-to-all-start.1 = ((bf16[16,32,512]{2,1,0:T(8,128)(2,1)}), bf16[16,32,512]{2,1,0:T(8,128)(2,1)S(1)}, u32[]{:S(2)}, u32[]{:S(2)}) async-start(bf16[16,32,512]{2,1,0:T(8,128)(2,1)} %get-tuple-element.30), calls=%async_computation.1 | async-start | bytes 1048576 | tf_op jit(solution)/shard_map/all_to_all | solution.py:393
  42.9 1.2 %collective-permute-done.7.crossed = bf16[8,32,512]{2,1,0:T(8,128)(2,1)S(1)} collective-permute-done((bf16[8,32,512]{2,1,0:T(8,128)(2,1)S(1)}, bf16[8,32,512]{2,1,0:T(8,128)(2,1)S(1)}, u32[]{:S(2)}, u32[]{:S(2)}) %collective-permute-start.7) | collective-permute-done | bytes 262176 | tf_op jit(solution)/shard_map/ppermute | solution.py:372
  44.1 3.4 %conv_rest.1 = (bf16[8,32,512]{2,1,0:T(8,128)(2,1)S(1)}, bf16[8,32,512]{2,1,0:T(8,128)(2,1)S(1)}) custom-call(f32[1,8192]{1,0:T(1,128)S(1)} %get-tuple-element.34.refs_8_.lag_row, bf16[8,32,512]{2,1,0:T(8,128)(2,1)S(1)} %collective-permute-done.7.crossed, bf16[2,32,512]{2,1,0:T(8,128)(2,1)S(1)} %copy-done, ...), custom_call_target="tpu_custom_call" | custom-call | flops 1000000 | bytes 100000 | tf_op jit(solution)/shard_map/conv_rest/pallas_call | solution.py:277
  48.0 1.2 %collective-permute-done.8.other = bf16[8,32,512]{2,1,0:T(8,128)(2,1)S(1)} collective-permute-done((bf16[8,32,512]{2,1,0:T(8,128)(2,1)S(1)}, bf16[8,32,512]{2,1,0:T(8,128)(2,1)S(1)}, u32[]{:S(2)}, u32[]{:S(2)}) %collective-permute-start.8) | collective-permute-done | bytes 262176 | tf_op jit(solution)/shard_map/ppermute | solution.py:372
  49.2 2.0 %collective-permute-start.9 = (bf16[2,32,512]{2,1,0:T(8,128)(2,1)S(1)}, bf16[2,32,512]{2,1,0:T(8,128)(2,1)S(1)}, u32[]{:S(2)}, u32[]{:S(2)}) collective-permute-start(bf16[2,32,512]{2,1,0:T(8,128)(2,1)S(1)} %get-tuple-element.46), channel_id=1, source_target_pairs={{0,2},{1,3},{2,0},{3,1},{4,6},{5,7},{6,4},{7,5},{8,10},{9,11},{10,... | collective-permute-start | bytes 196616 | tf_op jit(solution)/shard_map/ppermute | solution.py:378
  51.1 1.5 %collective-permute-start.10 = (bf16[2,32,512]{2,1,0:T(8,128)(2,1)S(1)}, bf16[2,32,512]{2,1,0:T(8,128)(2,1)S(1)}, u32[]{:S(2)}, u32[]{:S(2)}) collective-permute-start(bf16[2,32,512]{2,1,0:T(8,128)(2,1)S(1)} %get-tuple-element.47), channel_id=1, source_target_pairs={{0,4},{1,5},{2,6},{3,7},{4,0},{5,1},{6,2},{7,3},{8,12},{9,13},{10,... | collective-permute-start | bytes 196616 | tf_op jit(solution)/shard_map/ppermute | solution.py:378
  52.7 2.8 %collective-permute-start.12 = (bf16[2,32,512]{2,1,0:T(8,128)(2,1)S(1)}, bf16[2,32,512]{2,1,0:T(8,128)(2,1)S(1)}, u32[]{:S(2)}, u32[]{:S(2)}) collective-permute-start(bf16[2,32,512]{2,1,0:T(8,128)(2,1)S(1)} %get-tuple-element.49), channel_id=1, source_target_pairs={{0,8},{1,9},{2,10},{3,11},{4,12},{5,13},{6,14},{7,15},{8,0},{9,1},... | collective-permute-start | bytes 196616 | tf_op jit(solution)/shard_map/ppermute | solution.py:378
  55.5 1.5 %collective-permute-start.13 = (bf16[2,32,512]{2,1,0:T(8,128)(2,1)S(1)}, bf16[2,32,512]{2,1,0:T(8,128)(2,1)S(1)}, u32[]{:S(2)}, u32[]{:S(2)}) collective-permute-start(bf16[2,32,512]{2,1,0:T(8,128)(2,1)S(1)} %get-tuple-element.50), channel_id=1, source_target_pairs={{0,10},{1,11},{2,8},{3,9},{4,14},{5,15},{6,12},{7,13},{8,2},{9,3},... | collective-permute-start | bytes 196616 | tf_op jit(solution)/shard_map/ppermute | solution.py:378
  57.0 3.3 %collective-permute-start.14 = (bf16[2,32,512]{2,1,0:T(8,128)(2,1)S(1)}, bf16[2,32,512]{2,1,0:T(8,128)(2,1)S(1)}, u32[]{:S(2)}, u32[]{:S(2)}) collective-permute-start(bf16[2,32,512]{2,1,0:T(8,128)(2,1)S(1)} %get-tuple-element.51), channel_id=1, source_target_pairs={{0,12},{1,13},{2,14},{3,15},{4,8},{5,9},{6,10},{7,11},{8,4},{9,5},... | collective-permute-start | bytes 196616 | tf_op jit(solution)/shard_map/ppermute | solution.py:378
  60.4 1.6 %copy-done.2 = bf16[1024,1024]{1,0:T(8,128)(2,1)S(1)} copy-done((bf16[1024,1024]{1,0:T(8,128)(2,1)S(1)}, bf16[1024,1024]{1,0:T(8,128)(2,1)}, u32[]{:S(2)}) %copy-start.2) | copy-done | bytes 2097176
  62.0 1.2 %copy-done.3 = bf16[512,1024]{1,0:T(8,128)(2,1)S(1)} copy-done((bf16[512,1024]{1,0:T(8,128)(2,1)S(1)}, bf16[512,1024]{1,0:T(8,128)(2,1)}, u32[]{:S(2)}) %copy-start.3) | copy-done | bytes 1048600
  63.2 2.2 %mix_first.1 = (f32[512,1024]{1,0:T(8,128)S(1)}, f32[16,32,512]{2,1,0:T(8,128)S(1)}, bf16[16,32,1024]{2,1,0:T(8,128)(2,1)S(1)}) custom-call(bf16[512,1024]{1,0:T(8,128)(2,1)S(1)} %copy-done.3, bf16[1024,1024]{1,0:T(8,128)(2,1)S(1)} %copy-done.1, bf16[16,32,512]{2,1,0:T(8,128)(2,1)S(1)} %all-to-all-done.1.conv, bf16[1024,1024]{1,0:T(8,128)(2,1)S(1)} %copy-done.2), custom_call_target="tpu_custom_call" | custom-call | flops 2147483648 | bytes 4194304 | tf_op jit(solution)/shard_map/mix_first/pallas_call | solution.py:332
  65.5 0.9 %collective-permute-done.13.refs_5_ = bf16[2,32,512]{2,1,0:T(8,128)(2,1)S(1)} collective-permute-done((bf16[2,32,512]{2,1,0:T(8,128)(2,1)S(1)}, bf16[2,32,512]{2,1,0:T(8,128)(2,1)S(1)}, u32[]{:S(2)}, u32[]{:S(2)}) %collective-permute-start.13) | collective-permute-done | bytes 65568 | tf_op jit(solution)/shard_map/ppermute | solution.py:378
  66.3 1.0 %collective-permute-done.15.refs_7_ = bf16[2,32,512]{2,1,0:T(8,128)(2,1)S(1)} collective-permute-done((bf16[2,32,512]{2,1,0:T(8,128)(2,1)S(1)}, bf16[2,32,512]{2,1,0:T(8,128)(2,1)S(1)}, u32[]{:S(2)}, u32[]{:S(2)}) %collective-permute-start.15) | collective-permute-done | bytes 65568 | tf_op jit(solution)/shard_map/ppermute | solution.py:378
  67.3 1.8 %mix_rest.1 = bf16[512,1024]{1,0:T(8,128)(2,1)} custom-call(f32[512,1024]{1,0:T(8,128)S(1)} %get-tuple-element.31.partial, f32[16,32,512]{2,1,0:T(8,128)S(1)} %get-tuple-element.32.silu, bf16[16,32,1024]{2,1,0:T(8,128)(2,1)S(1)} %get-tuple-element.33.weight, bf16[2,32,512]{2,1,0:T(8,128)(2,1)S(1)} %get-tuple-element.45.refs_0_, ...), custom_call_target="tpu_custom_call" | custom-call | flops 536870912 | bytes 4194304 | tf_op jit(solution)/shard_map/mix_rest/pallas_call | solution.py:359
  (27 shorter events, 2.9 us)
Async XLA Ops:
  5.1 36.9 %copy-start = (bf16[2,32,512]{2,1,0:T(8,128)(2,1)S(1)}, bf16[2,32,512]{2,1,0:T(8,128)(2,1)}, u32[]{:S(2)}) copy-start(bf16[2,32,512]{2,1,0:T(8,128)(2,1)} %get-tuple-element.35.refs_0_) | copy-start | bytes 196612
  5.1 24.5 %all-to-all-start = ((bf16[16,144,128]{2,1,0:T(8,128)(2,1)}), bf16[16,144,128]{2,1,0:T(8,128)(2,1)S(1)}, u32[]{:S(2)}, u32[]{:S(2)}) async-start(bf16[16,144,128]{2,1,0:T(8,128)(2,1)} %get-tuple-element.29), calls=%async_computation | async-start | bytes 1179648 | tf_op jit(solution)/shard_map/all_to_all | solution.py:389
  12.6 8.0 %collective-permute-start = (bf16[2,32,512]{2,1,0:T(8,128)(2,1)}, bf16[2,32,512]{2,1,0:T(8,128)(2,1)S(1)}, u32[]{:S(2)}, u32[]{:S(2)}) collective-permute-start(bf16[2,32,512]{2,1,0:T(8,128)(2,1)} %get-tuple-element.36), channel_id=1, source_target_pairs={{0,2},{1,3},{2,0},{3,1},{4,6},{5,7},{6,4},{7,5},{8,10},{9,11},{10,... | collective-permute-start | bytes 196616 | tf_op jit(solution)/shard_map/ppermute | solution.py:378
  14.5 11.0 %collective-permute-start.1 = (bf16[2,32,512]{2,1,0:T(8,128)(2,1)}, bf16[2,32,512]{2,1,0:T(8,128)(2,1)S(1)}, u32[]{:S(2)}, u32[]{:S(2)}) collective-permute-start(bf16[2,32,512]{2,1,0:T(8,128)(2,1)} %get-tuple-element.37), channel_id=1, source_target_pairs={{0,4},{1,5},{2,6},{3,7},{4,0},{5,1},{6,2},{7,3},{8,12},{9,13},{10,... | collective-permute-start | bytes 196616 | tf_op jit(solution)/shard_map/ppermute | solution.py:378
  16.0 25.9 %collective-permute-start.2 = (bf16[2,32,512]{2,1,0:T(8,128)(2,1)}, bf16[2,32,512]{2,1,0:T(8,128)(2,1)S(1)}, u32[]{:S(2)}, u32[]{:S(2)}) collective-permute-start(bf16[2,32,512]{2,1,0:T(8,128)(2,1)} %get-tuple-element.38), channel_id=1, source_target_pairs={{0,6},{1,7},{2,4},{3,5},{4,2},{5,3},{6,0},{7,1},{8,14},{9,15},{10,... | collective-permute-start | bytes 196616 | tf_op jit(solution)/shard_map/ppermute | solution.py:378
  16.2 25.8 %collective-permute-start.3 = (bf16[2,32,512]{2,1,0:T(8,128)(2,1)}, bf16[2,32,512]{2,1,0:T(8,128)(2,1)S(1)}, u32[]{:S(2)}, u32[]{:S(2)}) collective-permute-start(bf16[2,32,512]{2,1,0:T(8,128)(2,1)} %get-tuple-element.39), channel_id=1, source_target_pairs={{0,8},{1,9},{2,10},{3,11},{4,12},{5,13},{6,14},{7,15},{8,0},{9,1},... | collective-permute-start | bytes 196616 | tf_op jit(solution)/shard_map/ppermute | solution.py:378
  18.9 23.0 %collective-permute-start.4 = (bf16[2,32,512]{2,1,0:T(8,128)(2,1)}, bf16[2,32,512]{2,1,0:T(8,128)(2,1)S(1)}, u32[]{:S(2)}, u32[]{:S(2)}) collective-permute-start(bf16[2,32,512]{2,1,0:T(8,128)(2,1)} %get-tuple-element.40), channel_id=1, source_target_pairs={{0,10},{1,11},{2,8},{3,9},{4,14},{5,15},{6,12},{7,13},{8,2},{9,3},... | collective-permute-start | bytes 196616 | tf_op jit(solution)/shard_map/ppermute | solution.py:378
  20.6 21.3 %collective-permute-start.5 = (bf16[2,32,512]{2,1,0:T(8,128)(2,1)}, bf16[2,32,512]{2,1,0:T(8,128)(2,1)S(1)}, u32[]{:S(2)}, u32[]{:S(2)}) collective-permute-start(bf16[2,32,512]{2,1,0:T(8,128)(2,1)} %get-tuple-element.41), channel_id=1, source_target_pairs={{0,12},{1,13},{2,14},{3,15},{4,8},{5,9},{6,10},{7,11},{8,4},{9,5},... | collective-permute-start | bytes 196616 | tf_op jit(solution)/shard_map/ppermute | solution.py:378
  25.6 16.4 %collective-permute-start.6 = (bf16[2,32,512]{2,1,0:T(8,128)(2,1)}, bf16[2,32,512]{2,1,0:T(8,128)(2,1)S(1)}, u32[]{:S(2)}, u32[]{:S(2)}) collective-permute-start(bf16[2,32,512]{2,1,0:T(8,128)(2,1)} %get-tuple-element.42), channel_id=1, source_target_pairs={{0,14},{1,15},{2,12},{3,13},{4,10},{5,11},{6,8},{7,9},{8,6},{9,7},... | collective-permute-start | bytes 196616 | tf_op jit(solution)/shard_map/ppermute | solution.py:378
  32.9 27.5 %all-to-all-start.1 = ((bf16[16,32,512]{2,1,0:T(8,128)(2,1)}), bf16[16,32,512]{2,1,0:T(8,128)(2,1)S(1)}, u32[]{:S(2)}, u32[]{:S(2)}) async-start(bf16[16,32,512]{2,1,0:T(8,128)(2,1)} %get-tuple-element.30), calls=%async_computation.1 | async-start | bytes 1048576 | tf_op jit(solution)/shard_map/all_to_all | solution.py:393
  42.0 18.4 %copy-start.1 = (bf16[1024,1024]{1,0:T(8,128)(2,1)S(1)}, bf16[1024,1024]{1,0:T(8,128)(2,1)}, u32[]{:S(2)}) copy-start(bf16[1024,1024]{1,0:T(8,128)(2,1)} %gate_weight.1) | copy-start | bytes 6291460
  42.5 1.6 %collective-permute-start.7 = (bf16[8,32,512]{2,1,0:T(8,128)(2,1)S(1)}, bf16[8,32,512]{2,1,0:T(8,128)(2,1)S(1)}, u32[]{:S(2)}, u32[]{:S(2)}) collective-permute-start(bf16[8,32,512]{2,1,0:T(8,128)(2,1)S(1)} %pack.1), channel_id=1, source_target_pairs={{0,1},{1,0},{2,3},{3,2},{4,5},{5,4},{6,7},{7,6},{8,9},{9,8},{10,11... | collective-permute-start | bytes 786440 | tf_op jit(solution)/shard_map/ppermute | solution.py:372
  47.5 1.6 %collective-permute-start.8 = (bf16[8,32,512]{2,1,0:T(8,128)(2,1)S(1)}, bf16[8,32,512]{2,1,0:T(8,128)(2,1)S(1)}, u32[]{:S(2)}, u32[]{:S(2)}) collective-permute-start(bf16[8,32,512]{2,1,0:T(8,128)(2,1)S(1)} %get-tuple-element.44), channel_id=1, source_target_pairs={{0,1},{1,0},{2,3},{3,2},{4,5},{5,4},{6,7},{7,6},{8,9},{9,8},{10,11... | collective-permute-start | bytes 786440 | tf_op jit(solution)/shard_map/ppermute | solution.py:372
  49.2 7.8 %collective-permute-start.9 = (bf16[2,32,512]{2,1,0:T(8,128)(2,1)S(1)}, bf16[2,32,512]{2,1,0:T(8,128)(2,1)S(1)}, u32[]{:S(2)}, u32[]{:S(2)}) collective-permute-start(bf16[2,32,512]{2,1,0:T(8,128)(2,1)S(1)} %get-tuple-element.46), channel_id=1, source_target_pairs={{0,2},{1,3},{2,0},{3,1},{4,6},{5,7},{6,4},{7,5},{8,10},{9,11},{10,... | collective-permute-start | bytes 196616 | tf_op jit(solution)/shard_map/ppermute | solution.py:378
  51.1 9.1 %collective-permute-start.10 = (bf16[2,32,512]{2,1,0:T(8,128)(2,1)S(1)}, bf16[2,32,512]{2,1,0:T(8,128)(2,1)S(1)}, u32[]{:S(2)}, u32[]{:S(2)}) collective-permute-start(bf16[2,32,512]{2,1,0:T(8,128)(2,1)S(1)} %get-tuple-element.47), channel_id=1, source_target_pairs={{0,4},{1,5},{2,6},{3,7},{4,0},{5,1},{6,2},{7,3},{8,12},{9,13},{10,... | collective-permute-start | bytes 196616 | tf_op jit(solution)/shard_map/ppermute | solution.py:378
  52.6 12.8 %collective-permute-start.11 = (bf16[2,32,512]{2,1,0:T(8,128)(2,1)S(1)}, bf16[2,32,512]{2,1,0:T(8,128)(2,1)S(1)}, u32[]{:S(2)}, u32[]{:S(2)}) collective-permute-start(bf16[2,32,512]{2,1,0:T(8,128)(2,1)S(1)} %get-tuple-element.48), channel_id=1, source_target_pairs={{0,6},{1,7},{2,4},{3,5},{4,2},{5,3},{6,0},{7,1},{8,14},{9,15},{10,... | collective-permute-start | bytes 196616 | tf_op jit(solution)/shard_map/ppermute | solution.py:378
  52.7 12.7 %collective-permute-start.12 = (bf16[2,32,512]{2,1,0:T(8,128)(2,1)S(1)}, bf16[2,32,512]{2,1,0:T(8,128)(2,1)S(1)}, u32[]{:S(2)}, u32[]{:S(2)}) collective-permute-start(bf16[2,32,512]{2,1,0:T(8,128)(2,1)S(1)} %get-tuple-element.49), channel_id=1, source_target_pairs={{0,8},{1,9},{2,10},{3,11},{4,12},{5,13},{6,14},{7,15},{8,0},{9,1},... | collective-permute-start | bytes 196616 | tf_op jit(solution)/shard_map/ppermute | solution.py:378
  55.5 10.8 %collective-permute-start.13 = (bf16[2,32,512]{2,1,0:T(8,128)(2,1)S(1)}, bf16[2,32,512]{2,1,0:T(8,128)(2,1)S(1)}, u32[]{:S(2)}, u32[]{:S(2)}) collective-permute-start(bf16[2,32,512]{2,1,0:T(8,128)(2,1)S(1)} %get-tuple-element.50), channel_id=1, source_target_pairs={{0,10},{1,11},{2,8},{3,9},{4,14},{5,15},{6,12},{7,13},{8,2},{9,3},... | collective-permute-start | bytes 196616 | tf_op jit(solution)/shard_map/ppermute | solution.py:378
  57.0 9.3 %collective-permute-start.14 = (bf16[2,32,512]{2,1,0:T(8,128)(2,1)S(1)}, bf16[2,32,512]{2,1,0:T(8,128)(2,1)S(1)}, u32[]{:S(2)}, u32[]{:S(2)}) collective-permute-start(bf16[2,32,512]{2,1,0:T(8,128)(2,1)S(1)} %get-tuple-element.51), channel_id=1, source_target_pairs={{0,12},{1,13},{2,14},{3,15},{4,8},{5,9},{6,10},{7,11},{8,4},{9,5},... | collective-permute-start | bytes 196616 | tf_op jit(solution)/shard_map/ppermute | solution.py:378
  60.3 7.1 %collective-permute-start.15 = (bf16[2,32,512]{2,1,0:T(8,128)(2,1)S(1)}, bf16[2,32,512]{2,1,0:T(8,128)(2,1)S(1)}, u32[]{:S(2)}, u32[]{:S(2)}) collective-permute-start(bf16[2,32,512]{2,1,0:T(8,128)(2,1)S(1)} %get-tuple-element.52), channel_id=1, source_target_pairs={{0,14},{1,15},{2,12},{3,13},{4,10},{5,11},{6,8},{7,9},{8,6},{9,7},... | collective-permute-start | bytes 196616 | tf_op jit(solution)/shard_map/ppermute | solution.py:378
  60.4 1.6 %copy-start.2 = (bf16[1024,1024]{1,0:T(8,128)(2,1)S(1)}, bf16[1024,1024]{1,0:T(8,128)(2,1)}, u32[]{:S(2)}) copy-start(bf16[1024,1024]{1,0:T(8,128)(2,1)} %weight.3) | copy-start | bytes 6291460
  62.0 1.2 %copy-start.3 = (bf16[512,1024]{1,0:T(8,128)(2,1)S(1)}, bf16[512,1024]{1,0:T(8,128)(2,1)}, u32[]{:S(2)}) copy-start(bf16[512,1024]{1,0:T(8,128)(2,1)} %tokens.3) | copy-start | bytes 3145732

commit v2 on v1

--- a/solution.py
+++ b/solution.py
@@ -35,92 +35,135 @@
     return me // 2, lax.rem(me, 2)
 
 
-def project_body(sizes, tokens, weight, lag_weight, lag_bias, *refs):
-    devices, per, first, heads, pieces = sizes
-    out, messages = refs[0], refs[1:-8]
-    tokens_here, weight_here, out_here, rest_here, token_done, weight_done, out_done, rest_done = refs[-8:]
-    rows, width = tokens.shape
+def load(tokens, weight, cuts, tokens_here, weight_here, done):
+    copies = [pltpu.make_async_copy(tokens, tokens_here, done.at[0])]
+    at = 0
+    for number, (start, size) in enumerate(cuts):
+        copies.append(
+            pltpu.make_async_copy(
+                weight.at[:, start : start + size], weight_here.at[:, at : at + size], done.at[number + 1]
+            )
+        )
+        at += size
+    return copies
+
+
+def load_scratch(rows, width, cuts):
+    return [
+        pltpu.VMEM((rows, width), bf16),
+        pltpu.VMEM((width, sum(size for _, size in cuts)), bf16),
+        pltpu.SemaphoreType.DMA((len(cuts) + 1,)),
+    ]
+
+
+def first_project_body(devices, channels, cuts, heads_of, tokens, weight, lag_weight, lag_bias, out, *refs):
+    tokens_here, weight_here, done, out_here, out_done = refs
+    rows = tokens.shape[0]
+    heads = lag_weight.shape[0]
     tiles = rows // LANES
-    step = width // pieces
-    count = step // per
-    reading, writing = [], []
-    for at in range(pieces):
-        cut = (slice(None), slice(step * at, step * at + step))
-        reading.append(pltpu.make_async_copy(weight.at[cut], weight_here.at[cut], weight_done.at[at]))
-        cut = slice(count * at, count * at + count)
-        writing.append(pltpu.make_async_copy(out_here.at[cut], out.at[cut], out_done.at[at]))
-    token_copy = pltpu.make_async_copy(tokens, tokens_here, token_done.at[0])
-    token_copy.start()
-    reading[0].start()
+    copies = load(tokens, weight, cuts, tokens_here, weight_here, done)
+    for copy in copies:
+        copy.start()
     square = (heads, heads)
     on_line = lax.broadcasted_iota(jnp.int32, square, 0) == lax.broadcasted_iota(jnp.int32, square, 1)
     bias = jnp.sum(jnp.where(on_line, jnp.broadcast_to(lag_bias[...], square), 0.0), axis=1, keepdims=True)
     lag_columns = lag_weight[...].T
-    token_copy.wait()
-    for copy in reading[1:]:
-        copy.start()
+    copies[0].wait()
     logits = jnp.dot(tokens_here[...], lag_columns, preferred_element_type=f32).T + bias
     lag_rows = jnp.tanh(logits) * (rows * devices) ** (-0.5)
-    chip, _ = place()
-    for at in range(pieces):
-        reading[at].wait()
-        part = jnp.dot(
-            tokens_here[...], weight_here[:, step * at : step * at + step], preferred_element_type=f32
-        )
-        part = part.astype(bf16).T
-        for group in range(count):
-            device = at * count + group
-            block = part[per * group : per * group + first]
-            for tile in range(tiles):
-                out_here[device, first * tile : first * tile + first] = block[
-                    :, LANES * tile : LANES * tile + LANES
-                ]
-            head = device * heads // devices
+    for copy in copies[1:]:
+        copy.wait()
+    part = jnp.dot(tokens_here[...], weight_here[...], preferred_element_type=f32).astype(bf16).T
+    writing = []
+    half = devices // 2
+    for device in range(devices):
+        block = part[channels * device : channels * device + channels]
+        for tile in range(tiles):
+            out_here[device, channels * tile : channels * tile + channels] = block[
+                :, LANES * tile : LANES * tile + LANES
+            ]
+        lines = []
+        for head in heads_of[device]:
             row = lag_rows[head : head + 1]
-            lines = [row[:, LANES * tile : LANES * tile + LANES] for tile in range(tiles)]
-            lines.append(jnp.zeros((out.shape[1] - first * tiles - tiles, LANES), f32))
-            out_here[device, first * tiles :] = jnp.concatenate(lines, axis=0).astype(bf16)
-        writing[at].start()
-        if first < per:
-            for group in range(count):
-                device = at * count + group
-                slot = jnp.bitwise_xor(chip, device // 2)
-                rest_here[slot, device % 2] = part[per * group + first : per * group + per]
-    for slot, message in enumerate(messages):
-        writing.append(pltpu.make_async_copy(rest_here.at[slot], message, rest_done.at[slot]))
-        writing[-1].start()
+            lines += [row[:, LANES * tile : LANES * tile + LANES] for tile in range(tiles)]
+        left = out.shape[1] - channels * tiles - len(lines)
+        if left:
+            lines.append(jnp.zeros((left, LANES), f32))
+        out_here[device, channels * tiles :] = jnp.concatenate(lines, axis=0).astype(bf16)
+        if device % half == half - 1:
+            cut = slice(device + 1 - half, device + 1)
+            writing.append(pltpu.make_async_copy(out_here.at[cut], out.at[cut], out_done.at[device // half]))
+            writing[-1].start()
     for copy in writing:
         copy.wait()
 
 
-def project(tokens, weight, lag_weight, lag_bias, devices, first):
+def first_project(tokens, weight, lag_weight, lag_bias, devices, channels, cuts, heads_of):
     rows, width = tokens.shape
     heads = lag_weight.shape[1]
-    per = width // devices
-    pieces = max(1, min(2, devices // 2))
-    tall = first * (rows // LANES) + TILE
-    outs = [shape_of((devices, tall, LANES))]
-    if first < per:
-        outs += [shape_of((2, per - first, rows))] * (devices // 2)
-    return pl.pallas_call(
-        functools.partial(project_body, (devices, per, first, heads, pieces)),
-        out_shape=outs,
+    out = (devices, channels * (rows // LANES) + 8, LANES)
+    return pl.pallas_call(
+        functools.partial(first_project_body, devices, channels, cuts, heads_of),
+        out_shape=shape_of(out),
         in_specs=[HBM, HBM, VMEM, VMEM],
-        out_specs=[HBM] * len(outs),
-        scratch_shapes=[
-            pltpu.VMEM((rows, width), bf16),
-            pltpu.VMEM((width, width), bf16),
-            pltpu.VMEM((devices, tall, LANES), bf16),
-            pltpu.VMEM((devices // 2, 2, max(per - first, TILE), rows), bf16),
-            pltpu.SemaphoreType.DMA((1,)),
-            pltpu.SemaphoreType.DMA((pieces,)),
-            pltpu.SemaphoreType.DMA((pieces,)),
-            pltpu.SemaphoreType.DMA((devices // 2,)),
-        ],
+        out_specs=HBM,
+        scratch_shapes=load_scratch(rows, width, cuts)
+        + [pltpu.VMEM(out, bf16), pltpu.SemaphoreType.DMA((2,))],
         compiler_params=LARGE,
         cost_estimate=cost(2 * rows * width * width, 4 * rows * width + 2 * width * width),
-        name="project",
+        name="project_first",
     )(tokens, weight, lag_weight.T, lag_bias.reshape(1, heads))
+
+
+def rest_project_body(channels, cuts, tokens, weight, keep, other, *refs):
+    tokens_here, weight_here, done = refs
+    copies = load(tokens, weight, cuts, tokens_here, weight_here, done)
+    for copy in copies:
+        copy.start()
+    for copy in copies:
+        copy.wait()
+    part = jnp.dot(tokens_here[...], weight_here[...], preferred_element_type=f32).astype(bf16).T
+    chip, core = place()
+    for there in range(keep.shape[0]):
+        low = part[2 * channels * there : 2 * channels * there + channels]
+        high = part[2 * channels * there + channels : 2 * channels * there + 2 * channels]
+        slot = jnp.bitwise_xor(chip, there)
+        keep[slot] = jnp.where(core == 0, low, high)
+        other[slot] = jnp.where(core == 0, high, low)
+
+
+def rest_project(tokens, weight, chips, channels, cuts):
+    rows, width = tokens.shape
+    half = (chips, channels, rows)
+    return pl.pallas_call(
+        functools.partial(rest_project_body, channels, cuts),
+        out_shape=[shape_of(half)] * 2,
+        in_specs=[HBM, HBM],
+        out_specs=[VMEM] * 2,
+        scratch_shapes=load_scratch(rows, width, cuts),
+        compiler_params=SMALL,
+        cost_estimate=cost(rows * width * width, 4 * rows * width),
+        name="project_rest",
+    )(tokens, weight)
+
+
+def meet_body(keep, other, *messages):
+    _, core = place()
+    for slot, message in enumerate(messages):
+        message[core] = keep[slot]
+        message[1 - core] = other[slot]
+
+
+def meet(keep, other):
+    chips, channels, rows = keep.shape
+    return pl.pallas_call(
+        meet_body,
+        out_shape=[shape_of((2, channels, rows))] * chips,
+        in_specs=[VMEM] * 2,
+        out_specs=[VMEM] * chips,
+        compiler_params=SMALL,
+        name="meet",
+    )(keep, other)
 
 
 def fill_strips(row, plus, minus):
@@ -175,12 +218,13 @@
     count, tall, _ = values.shape
     span = out.shape[2]
     tiles = span // LANES
-    pieces = []
+    own, later = [], []
     for at in range(count):
         rows = values[at, channels * tiles :].astype(f32)
-        pieces += [rows[tile : tile + 1] for tile in range(tiles)]
-    lag_row[...] = jnp.concatenate(pieces, axis=1)
-    fill_strips(lag_row[...], plus, minus)
+        own += [rows[tile : tile + 1] for tile in range(tiles)]
+        later += [rows[tiles + tile : tiles + tile + 1] for tile in range(tiles)]
+    lag_row[...] = jnp.concatenate(later, axis=1)
+    fill_strips(jnp.concatenate(own, axis=1), plus, minus)
 
     def block_of(at):
         return jnp.concatenate(
@@ -216,33 +260,7 @@
     )(values)
 
 
-def pack_body(chips, *refs):
-    messages, out, done = refs[:chips], refs[-2], refs[-1]
-    core = 1 - place()[1]
-    copies = [
-        pltpu.make_async_copy(messages[slot].at[core], out.at[slot], done.at[slot]) for slot in range(chips)
-    ]
-    for copy in copies:
-        copy.start()
-    for copy in copies:
-        copy.wait()
-
-
-def pack(messages, after):
-    chips = len(messages)
-    return pl.pallas_call(
-        functools.partial(pack_body, chips),
-        out_shape=shape_of((chips,) + messages[0].shape[1:]),
-        in_specs=[HBM] * (chips + 1),
-        out_specs=VMEM,
-        scratch_shapes=[pltpu.SemaphoreType.DMA((chips,))],
-        compiler_params=SMALL,
-        cost_estimate=cost(6e10, 1e8),
-        name="pack",
-    )(*messages, after)
-
-
-def rest_body(lag_row, crossed, *refs):
+def rest_body(lag_row, *refs):
     chips = len(refs) - 10
     messages, keep, other = refs[:chips], refs[chips], refs[chips + 1]
     gathered, done, *scratch = refs[chips + 2 :]
@@ -251,11 +269,9 @@
     copies = []
     for slot, message in enumerate(messages):
         base = 2 * jnp.bitwise_xor(chip, slot)
-        copies.append(pltpu.make_async_copy(message.at[core], gathered.at[base + core], done.at[slot]))
+        copies.append(pltpu.make_async_copy(message, gathered.at[pl.ds(base, 2)], done.at[slot]))
         copies[-1].start()
     fill_strips(lag_row[...], plus, minus)
-    for slot in range(chips):
-        gathered[2 * jnp.bitwise_xor(chip, slot) + 1 - core] = crossed[slot]
     for copy in copies:
         copy.wait()
     convolve(lambda at: gathered[at], *scratch)
@@ -270,21 +286,21 @@
         other[slot] = gathered[base + 1 - core]
 
 
-def convolve_rest(lag_row, crossed, messages):
+def convolve_rest(lag_row, messages):
     chips = len(messages)
     _, channels, span = messages[0].shape
     result = shape_of((chips, channels, span))
     return pl.pallas_call(
         rest_body,
         out_shape=[result] * 2,
-        in_specs=[VMEM] * 2 + [HBM] * chips,
+        in_specs=[VMEM] + [HBM] * chips,
         out_specs=[VMEM] * 2,
         scratch_shapes=[pltpu.VMEM((2 * chips, channels, span), bf16), pltpu.SemaphoreType.DMA((chips,))]
         + scratch_for(2 * chips, channels, span),
         compiler_params=SMALL,
-        cost_estimate=cost(1e6, 1e5),
+        cost_estimate=cost(6e10, 1e8),
         name="conv_rest",
-    )(lag_row, crossed, *messages)
+    )(lag_row, *messages)
 
 
 def join_body(keep, other, *messages):
@@ -310,16 +326,18 @@
     width, columns = weight.shape
     per = width // devices
     gate = jnp.dot(tokens[...], gate_weight[...], preferred_element_type=f32)
-    silu = (gate / (1.0 + jnp.exp(-gate))).T.reshape(devices, per, rows)
-    used = weight[...].reshape(devices, per, columns)
-    gated = (conv[...].astype(f32) * silu[:, :first]).astype(bf16).reshape(devices * first, rows)
-    mixed = jnp.dot(
-        gated.T, used[:, :first].reshape(devices * first, columns), preferred_element_type=f32
-    )
+    silu = (gate / (1.0 + jnp.exp(-gate))).T
+    used = weight[...]
+    if late:
+        silu = silu.reshape(devices // 4, 4 * per, rows)
+        used = used.reshape(devices // 4, 4 * per, columns)
+        late[0][...] = silu[:, 4 * first :].reshape(late[0].shape)
+        late[1][...] = used[:, 4 * first :].reshape(late[1].shape)
+        silu = silu[:, : 4 * first]
+        used = used[:, : 4 * first].reshape(devices * first, columns)
+    gated = (conv[...].astype(f32) * silu.reshape(devices, first, rows)).astype(bf16)
+    mixed = jnp.dot(gated.reshape(devices * first, rows).T, used, preferred_element_type=f32)
     out[...] = mixed.astype(out.dtype)
-    if late:
-        late[0][...] = silu[:, first:]
-        late[1][...] = used[:, first:]
 
 
 def mix_first(tokens, gate_weight, conv, weight):
@@ -383,18 +401,33 @@
     rows, width = tokens.shape
     devices = lax.axis_size("seq")
     per = width // devices
-    splits = per % (2 * TILE) == 0 and devices & (devices - 1) == 0
-    first = per // 2 if splits else per
-    blocks, *rest = project(tokens, value_weight, kernel_weight, kernel_bias, devices, first)
+    heads = kernel_weight.shape[1]
+    splits = per % (2 * TILE) == 0 and devices & (devices - 1) == 0 and devices % 4 == 0
+    splits = splits and heads == devices and 2 * per % LANES == 0
+    if splits:
+        first = per // 2
+        span = 4 * per
+        cuts = [(span * at, span // 2) for at in range(devices // 4)]
+        later = [(start + size, size) for start, size in cuts]
+        pairs = [(at // 4 * 4 + at % 4 // 2, at // 4 * 4 + 2 + at % 4 // 2) for at in range(devices)]
+        blocks = first_project(
+            tokens, value_weight, kernel_weight, kernel_bias, devices, first, cuts, pairs
+        )
+    else:
+        first = per
+        alone = [(at * heads // devices,) for at in range(devices)]
+        blocks = first_project(
+            tokens, value_weight, kernel_weight, kernel_bias, devices, first, [(0, width)], alone
+        )
     columns = lax.all_to_all(blocks, "seq", split_axis=0, concat_axis=0, tiled=True)
     if splits:
-        messages = to_chips(rest, devices)
+        keep, other = rest_project(tokens, value_weight, devices // 2, per - first, later)
+        messages = to_chips(meet(keep, to_core(other, devices)), devices)
     convolved, lag_row = convolve_first(columns, first, rows)
     returned = lax.all_to_all(convolved, "seq", split_axis=0, concat_axis=0, tiled=True)
     if not splits:
         return mix_first(tokens, gate_weight, returned, out_weight)[0]
-    crossed = to_core(pack(messages, lag_row), devices)
-    keep, other = convolve_rest(lag_row, crossed, messages)
+    keep, other = convolve_rest(lag_row, messages)
     messages = to_chips(join(keep, to_core(other, devices)), devices)
     return mix_rest(*mix_first(tokens, gate_weight, returned, out_weight), messages)
 

time: 69.6 us -> 67.6 us (0.971)
  starting transfers between devices: 44.6 us -> 40.8 us
  local copies, waits for them, and re-layouts: 2.83 us -> 4.77 us
    ppermute x14, starting transfers between devices: 27.2 us -> 23.5 us  [to_chips(): lax.ppermute(messages[slot], 'seq', [(i, i ^ 2 * slot) for i in range(dev...]
    unnamed x8, local copies, waits for them, and re-layouts: 2.83 us -> 4.77 us
    pallas_call x3 -> x4, Pallas kernels: 8.93 us -> 9.23 us  [the longest x1 4.19 us: first_project(): pl.pallas_call(functools.partial(first_project_body, devices, channels, c...]
  transfers between devices with their start and end apart: 18 -> 18, of which waited for: 6 -> 3; matrix products, arithmetic and copies ran while one was open for 0% -> 0% of each run, Pallas kernels for 14% -> 16%
where the time goes in v2:
time: 67.6 us; the launch traced here: 67.1 us
  starting transfers between devices  40.8 us (60%)
  Pallas kernels  16.5 us (24%)
  waiting for transfers between devices  4.91 us (7%)
  local copies, waits for them, and re-layouts  4.77 us (7%)
    ppermute x14, starting transfers between devices, to_chips(): lax.ppermute(messages[slot], 'seq', [(i, i ^ 2 * slot) for i in range(dev...  23.5 us
    all_to_all x1, starting transfers between devices, body(): lax.all_to_all(convolved, 'seq', split_axis=0, concat_axis=0, tiled=True)  8.95 us
    all_to_all x1, starting transfers between devices, body(): lax.all_to_all(blocks, 'seq', split_axis=0, concat_axis=0, tiled=True)  7.4 us
    unnamed x8, local copies, waits for them, and re-layouts  4.77 us
    pallas_call x1, Pallas kernels, first_project(): pl.pallas_call(functools.partial(first_project_body, devices, channels, c...  4.19 us
    pallas_call x1, Pallas kernels, convolve_rest(): pl.pallas_call(rest_body, out_shape=[result] * 2, in_specs=[VMEM] + [HBM]...  3.8 us
    pallas_call x1, Pallas kernels, convolve_first(): pl.pallas_call(functools.partial(first_body, channels), out_shape=[shape_...  3.33 us
    ppermute x14, waiting for transfers between devices, to_chips(): lax.ppermute(messages[slot], 'seq', [(i, i ^ 2 * slot) for i in range(dev...  2.58 us
  transfers between devices with their start and end apart: 18, of which 3 were waited for; matrix products, arithmetic and copies ran while one was open for 0% of the time, Pallas kernels for 16%

profile of v2, /device:TPU:0, one launch (start us, length us, event | category | flops | bytes accessed | tf_op | source)
XLA Modules:
  0.0 67.1 jit_solution(14034989477566101843)
XLA Ops:
  0.0 4.2 %project_first.1 = bf16[16,136,128]{2,1,0:T(8,128)(2,1)} custom-call(bf16[512,1024]{1,0:T(8,128)(2,1)} %tokens.5, bf16[1024,1024]{1,0:T(8,128)(2,1)} %weight.5, bf16[16,1024]{1,0:T(8,128)(2,1)} %bitcast.2, f32[1,16]{1,0:T(1,128)} %bitcast.3), custom_call_target="tpu_custom_call" | custom-call | flops 1073741824 | bytes 4194304 | tf_op jit(solution)/shard_map/project_first/pallas_call | solution.py:105
  4.2 7.4 %all-to-all-start = ((bf16[16,136,128]{2,1,0:T(8,128)(2,1)}), bf16[16,136,128]{2,1,0:T(8,128)(2,1)S(1)}, u32[]{:S(2)}, u32[]{:S(2)}) async-start(bf16[16,136,128]{2,1,0:T(8,128)(2,1)} %project_first.1), calls=%async_computation | async-start | bytes 1114112 | tf_op jit(solution)/shard_map/all_to_all | solution.py:422
  11.6 1.6 %copy-done = bf16[1024,1024]{1,0:T(8,128)(2,1)S(1)} copy-done((bf16[1024,1024]{1,0:T(8,128)(2,1)S(1)}, bf16[1024,1024]{1,0:T(8,128)(2,1)}, u32[]{:S(2)}) %copy-start) | copy-done | bytes 2097176
  13.2 1.2 %project_rest.1 = (bf16[8,32,512]{2,1,0:T(8,128)(2,1)S(1)}, bf16[8,32,512]{2,1,0:T(8,128)(2,1)S(1)}) custom-call(bf16[512,1024]{1,0:T(8,128)(2,1)S(1)} %copy-done.1, bf16[1024,1024]{1,0:T(8,128)(2,1)S(1)} %copy-done), custom_call_target="tpu_custom_call" | custom-call | flops 536870912 | bytes 2097152 | tf_op jit(solution)/shard_map/project_rest/pallas_call | solution.py:138
  14.9 1.2 %collective-permute-done.other = bf16[8,32,512]{2,1,0:T(8,128)(2,1)S(1)} collective-permute-done((bf16[8,32,512]{2,1,0:T(8,128)(2,1)S(1)}, bf16[8,32,512]{2,1,0:T(8,128)(2,1)S(1)}, u32[]{:S(2)}, u32[]{:S(2)}) %collective-permute-start) | collective-permute-done | bytes 262176 | tf_op jit(solution)/shard_map/ppermute | solution.py:390
  16.1 2.0 %collective-permute-start.1 = (bf16[2,32,512]{2,1,0:T(8,128)(2,1)S(1)}, bf16[2,32,512]{2,1,0:T(8,128)(2,1)S(1)}, u32[]{:S(2)}, u32[]{:S(2)}) collective-permute-start(bf16[2,32,512]{2,1,0:T(8,128)(2,1)S(1)} %get-tuple-element.38), channel_id=1, source_target_pairs={{0,2},{1,3},{2,0},{3,1},{4,6},{5,7},{6,4},{7,5},{8,10},{9,11},{10,... | collective-permute-start | bytes 196616 | tf_op jit(solution)/shard_map/ppermute | solution.py:396
  18.0 1.5 %collective-permute-start.2 = (bf16[2,32,512]{2,1,0:T(8,128)(2,1)S(1)}, bf16[2,32,512]{2,1,0:T(8,128)(2,1)S(1)}, u32[]{:S(2)}, u32[]{:S(2)}) collective-permute-start(bf16[2,32,512]{2,1,0:T(8,128)(2,1)S(1)} %get-tuple-element.39), channel_id=1, source_target_pairs={{0,4},{1,5},{2,6},{3,7},{4,0},{5,1},{6,2},{7,3},{8,12},{9,13},{10,... | collective-permute-start | bytes 196616 | tf_op jit(solution)/shard_map/ppermute | solution.py:396
  19.7 2.8 %collective-permute-start.4 = (bf16[2,32,512]{2,1,0:T(8,128)(2,1)S(1)}, bf16[2,32,512]{2,1,0:T(8,128)(2,1)S(1)}, u32[]{:S(2)}, u32[]{:S(2)}) collective-permute-start(bf16[2,32,512]{2,1,0:T(8,128)(2,1)S(1)} %get-tuple-element.41), channel_id=1, source_target_pairs={{0,8},{1,9},{2,10},{3,11},{4,12},{5,13},{6,14},{7,15},{8,0},{9,1},... | collective-permute-start | bytes 196616 | tf_op jit(solution)/shard_map/ppermute | solution.py:396
  22.4 1.5 %collective-permute-start.5 = (bf16[2,32,512]{2,1,0:T(8,128)(2,1)S(1)}, bf16[2,32,512]{2,1,0:T(8,128)(2,1)S(1)}, u32[]{:S(2)}, u32[]{:S(2)}) collective-permute-start(bf16[2,32,512]{2,1,0:T(8,128)(2,1)S(1)} %get-tuple-element.42), channel_id=1, source_target_pairs={{0,10},{1,11},{2,8},{3,9},{4,14},{5,15},{6,12},{7,13},{8,2},{9,3},... | collective-permute-start | bytes 196616 | tf_op jit(solution)/shard_map/ppermute | solution.py:396
  23.9 3.3 %collective-permute-start.6 = (bf16[2,32,512]{2,1,0:T(8,128)(2,1)S(1)}, bf16[2,32,512]{2,1,0:T(8,128)(2,1)S(1)}, u32[]{:S(2)}, u32[]{:S(2)}) collective-permute-start(bf16[2,32,512]{2,1,0:T(8,128)(2,1)S(1)} %get-tuple-element.43), channel_id=1, source_target_pairs={{0,12},{1,13},{2,14},{3,15},{4,8},{5,9},{6,10},{7,11},{8,4},{9,5},... | collective-permute-start | bytes 196616 | tf_op jit(solution)/shard_map/ppermute | solution.py:396
  28.0 3.3 %conv_first.1 = (bf16[16,32,512]{2,1,0:T(8,128)(2,1)}, f32[1,8192]{1,0:T(1,128)S(1)}) custom-call(bf16[16,136,128]{2,1,0:T(8,128)(2,1)S(1)} %all-to-all-done.values), custom_call_target="tpu_custom_call" | custom-call | flops 1000000 | bytes 100000 | tf_op jit(solution)/shard_map/conv_first/pallas_call | solution.py:251
  31.3 9.0 %all-to-all-start.1 = ((bf16[16,32,512]{2,1,0:T(8,128)(2,1)}), bf16[16,32,512]{2,1,0:T(8,128)(2,1)S(1)}, u32[]{:S(2)}, u32[]{:S(2)}) async-start(bf16[16,32,512]{2,1,0:T(8,128)(2,1)} %get-tuple-element.30), calls=%async_computation.1 | async-start | bytes 1048576 | tf_op jit(solution)/shard_map/all_to_all | solution.py:427
  40.3 3.8 %conv_rest.1 = (bf16[8,32,512]{2,1,0:T(8,128)(2,1)S(1)}, bf16[8,32,512]{2,1,0:T(8,128)(2,1)S(1)}) custom-call(f32[1,8192]{1,0:T(1,128)S(1)} %get-tuple-element.34.lag_row, bf16[2,32,512]{2,1,0:T(8,128)(2,1)S(1)} %get-tuple-element.37.refs_0_, bf16[2,32,512]{2,1,0:T(8,128)(2,1)S(1)} %collective-permute-done.1.refs_1_, ...), custom_call_target="tpu_custom_call" | custom-call | flops 60000002048 | bytes 100000000 | tf_op jit(solution)/shard_map/conv_rest/pallas_call | solution.py:293
  44.6 1.2 %collective-permute-done.8.other = bf16[8,32,512]{2,1,0:T(8,128)(2,1)S(1)} collective-permute-done((bf16[8,32,512]{2,1,0:T(8,128)(2,1)S(1)}, bf16[8,32,512]{2,1,0:T(8,128)(2,1)S(1)}, u32[]{:S(2)}, u32[]{:S(2)}) %collective-permute-start.8) | collective-permute-done | bytes 262176 | tf_op jit(solution)/shard_map/ppermute | solution.py:390
  45.8 2.0 %collective-permute-start.9 = (bf16[2,32,512]{2,1,0:T(8,128)(2,1)S(1)}, bf16[2,32,512]{2,1,0:T(8,128)(2,1)S(1)}, u32[]{:S(2)}, u32[]{:S(2)}) collective-permute-start(bf16[2,32,512]{2,1,0:T(8,128)(2,1)S(1)} %get-tuple-element.48), channel_id=1, source_target_pairs={{0,2},{1,3},{2,0},{3,1},{4,6},{5,7},{6,4},{7,5},{8,10},{9,11},{10,... | collective-permute-start | bytes 196616 | tf_op jit(solution)/shard_map/ppermute | solution.py:396
  47.7 1.5 %collective-permute-start.10 = (bf16[2,32,512]{2,1,0:T(8,128)(2,1)S(1)}, bf16[2,32,512]{2,1,0:T(8,128)(2,1)S(1)}, u32[]{:S(2)}, u32[]{:S(2)}) collective-permute-start(bf16[2,32,512]{2,1,0:T(8,128)(2,1)S(1)} %get-tuple-element.49), channel_id=1, source_target_pairs={{0,4},{1,5},{2,6},{3,7},{4,0},{5,1},{6,2},{7,3},{8,12},{9,13},{10,... | collective-permute-start | bytes 196616 | tf_op jit(solution)/shard_map/ppermute | solution.py:396
  49.4 2.8 %collective-permute-start.12 = (bf16[2,32,512]{2,1,0:T(8,128)(2,1)S(1)}, bf16[2,32,512]{2,1,0:T(8,128)(2,1)S(1)}, u32[]{:S(2)}, u32[]{:S(2)}) collective-permute-start(bf16[2,32,512]{2,1,0:T(8,128)(2,1)S(1)} %get-tuple-element.51), channel_id=1, source_target_pairs={{0,8},{1,9},{2,10},{3,11},{4,12},{5,13},{6,14},{7,15},{8,0},{9,1},... | collective-permute-start | bytes 196616 | tf_op jit(solution)/shard_map/ppermute | solution.py:396
  52.1 1.5 %collective-permute-start.13 = (bf16[2,32,512]{2,1,0:T(8,128)(2,1)S(1)}, bf16[2,32,512]{2,1,0:T(8,128)(2,1)S(1)}, u32[]{:S(2)}, u32[]{:S(2)}) collective-permute-start(bf16[2,32,512]{2,1,0:T(8,128)(2,1)S(1)} %get-tuple-element.52), channel_id=1, source_target_pairs={{0,10},{1,11},{2,8},{3,9},{4,14},{5,15},{6,12},{7,13},{8,2},{9,3},... | collective-permute-start | bytes 196616 | tf_op jit(solution)/shard_map/ppermute | solution.py:396
  53.6 3.3 %collective-permute-start.14 = (bf16[2,32,512]{2,1,0:T(8,128)(2,1)S(1)}, bf16[2,32,512]{2,1,0:T(8,128)(2,1)S(1)}, u32[]{:S(2)}, u32[]{:S(2)}) collective-permute-start(bf16[2,32,512]{2,1,0:T(8,128)(2,1)S(1)} %get-tuple-element.53), channel_id=1, source_target_pairs={{0,12},{1,13},{2,14},{3,15},{4,8},{5,9},{6,10},{7,11},{8,4},{9,5},... | collective-permute-start | bytes 196616 | tf_op jit(solution)/shard_map/ppermute | solution.py:396
  57.5 1.6 %copy-done.2 = bf16[1024,1024]{1,0:T(8,128)(2,1)S(1)} copy-done((bf16[1024,1024]{1,0:T(8,128)(2,1)S(1)}, bf16[1024,1024]{1,0:T(8,128)(2,1)}, u32[]{:S(2)}) %copy-start.2) | copy-done | bytes 2097176
  59.1 1.6 %copy-done.3 = bf16[1024,1024]{1,0:T(8,128)(2,1)S(1)} copy-done((bf16[1024,1024]{1,0:T(8,128)(2,1)S(1)}, bf16[1024,1024]{1,0:T(8,128)(2,1)}, u32[]{:S(2)}) %copy-start.3) | copy-done | bytes 2097176
  60.7 2.1 %mix_first.1 = (f32[512,1024]{1,0:T(8,128)S(1)}, f32[16,32,512]{2,1,0:T(8,128)S(1)}, bf16[16,32,1024]{2,1,0:T(8,128)(2,1)S(1)}) custom-call(bf16[512,1024]{1,0:T(8,128)(2,1)S(1)} %copy-done.1, bf16[1024,1024]{1,0:T(8,128)(2,1)S(1)} %copy-done.2, bf16[16,32,512]{2,1,0:T(8,128)(2,1)S(1)} %all-to-all-done.1.conv, bf16[1024,1024]{1,0:T(8,128)(2,1)S(1)} %copy-done.3), custom_call_target="tpu_custom_call" | custom-call | flops 2147483648 | bytes 4194304 | tf_op jit(solution)/shard_map/mix_first/pallas_call | solution.py:350
  62.8 2.5 %collective-permute-done.13.refs_5_ = bf16[2,32,512]{2,1,0:T(8,128)(2,1)S(1)} collective-permute-done((bf16[2,32,512]{2,1,0:T(8,128)(2,1)S(1)}, bf16[2,32,512]{2,1,0:T(8,128)(2,1)S(1)}, u32[]{:S(2)}, u32[]{:S(2)}) %collective-permute-start.13) | collective-permute-done | bytes 65568 | tf_op jit(solution)/shard_map/ppermute | solution.py:396
  65.3 1.8 %mix_rest.1 = bf16[512,1024]{1,0:T(8,128)(2,1)} custom-call(f32[512,1024]{1,0:T(8,128)S(1)} %get-tuple-element.31.partial, f32[16,32,512]{2,1,0:T(8,128)S(1)} %get-tuple-element.32.silu, bf16[16,32,1024]{2,1,0:T(8,128)(2,1)S(1)} %get-tuple-element.33.weight, bf16[2,32,512]{2,1,0:T(8,128)(2,1)S(1)} %get-tuple-element.47.refs_0_, ...), custom_call_target="tpu_custom_call" | custom-call | flops 536870912 | bytes 4194304 | tf_op jit(solution)/shard_map/mix_rest/pallas_call | solution.py:377
  (28 shorter events, 2.8 us)
Async XLA Ops:
  0.0 11.6 %copy-start.1 = (bf16[512,1024]{1,0:T(8,128)(2,1)S(1)}, bf16[512,1024]{1,0:T(8,128)(2,1)}, u32[]{:S(2)}) copy-start(bf16[512,1024]{1,0:T(8,128)(2,1)} %tokens.5) | copy-start | bytes 3145732
  4.2 23.8 %all-to-all-start = ((bf16[16,136,128]{2,1,0:T(8,128)(2,1)}), bf16[16,136,128]{2,1,0:T(8,128)(2,1)S(1)}, u32[]{:S(2)}, u32[]{:S(2)}) async-start(bf16[16,136,128]{2,1,0:T(8,128)(2,1)} %project_first.1), calls=%async_computation | async-start | bytes 1114112 | tf_op jit(solution)/shard_map/all_to_all | solution.py:422
  11.6 1.6 %copy-start = (bf16[1024,1024]{1,0:T(8,128)(2,1)S(1)}, bf16[1024,1024]{1,0:T(8,128)(2,1)}, u32[]{:S(2)}) copy-start(bf16[1024,1024]{1,0:T(8,128)(2,1)} %weight.5) | copy-start | bytes 6291460
  14.4 1.6 %collective-permute-start = (bf16[8,32,512]{2,1,0:T(8,128)(2,1)S(1)}, bf16[8,32,512]{2,1,0:T(8,128)(2,1)S(1)}, u32[]{:S(2)}, u32[]{:S(2)}) collective-permute-start(bf16[8,32,512]{2,1,0:T(8,128)(2,1)S(1)} %get-tuple-element.36), channel_id=1, source_target_pairs={{0,1},{1,0},{2,3},{3,2},{4,5},{5,4},{6,7},{7,6},{8,9},{9,8},{10,11... | collective-permute-start | bytes 786440 | tf_op jit(solution)/shard_map/ppermute | solution.py:390
  16.1 7.8 %collective-permute-start.1 = (bf16[2,32,512]{2,1,0:T(8,128)(2,1)S(1)}, bf16[2,32,512]{2,1,0:T(8,128)(2,1)S(1)}, u32[]{:S(2)}, u32[]{:S(2)}) collective-permute-start(bf16[2,32,512]{2,1,0:T(8,128)(2,1)S(1)} %get-tuple-element.38), channel_id=1, source_target_pairs={{0,2},{1,3},{2,0},{3,1},{4,6},{5,7},{6,4},{7,5},{8,10},{9,11},{10,... | collective-permute-start | bytes 196616 | tf_op jit(solution)/shard_map/ppermute | solution.py:396
  18.0 9.1 %collective-permute-start.2 = (bf16[2,32,512]{2,1,0:T(8,128)(2,1)S(1)}, bf16[2,32,512]{2,1,0:T(8,128)(2,1)S(1)}, u32[]{:S(2)}, u32[]{:S(2)}) collective-permute-start(bf16[2,32,512]{2,1,0:T(8,128)(2,1)S(1)} %get-tuple-element.39), channel_id=1, source_target_pairs={{0,4},{1,5},{2,6},{3,7},{4,0},{5,1},{6,2},{7,3},{8,12},{9,13},{10,... | collective-permute-start | bytes 196616 | tf_op jit(solution)/shard_map/ppermute | solution.py:396
  19.5 20.7 %collective-permute-start.3 = (bf16[2,32,512]{2,1,0:T(8,128)(2,1)S(1)}, bf16[2,32,512]{2,1,0:T(8,128)(2,1)S(1)}, u32[]{:S(2)}, u32[]{:S(2)}) collective-permute-start(bf16[2,32,512]{2,1,0:T(8,128)(2,1)S(1)} %get-tuple-element.40), channel_id=1, source_target_pairs={{0,6},{1,7},{2,4},{3,5},{4,2},{5,3},{6,0},{7,1},{8,14},{9,15},{10,... | collective-permute-start | bytes 196616 | tf_op jit(solution)/shard_map/ppermute | solution.py:396
  19.7 20.6 %collective-permute-start.4 = (bf16[2,32,512]{2,1,0:T(8,128)(2,1)S(1)}, bf16[2,32,512]{2,1,0:T(8,128)(2,1)S(1)}, u32[]{:S(2)}, u32[]{:S(2)}) collective-permute-start(bf16[2,32,512]{2,1,0:T(8,128)(2,1)S(1)} %get-tuple-element.41), channel_id=1, source_target_pairs={{0,8},{1,9},{2,10},{3,11},{4,12},{5,13},{6,14},{7,15},{8,0},{9,1},... | collective-permute-start | bytes 196616 | tf_op jit(solution)/shard_map/ppermute | solution.py:396
  22.4 17.8 %collective-permute-start.5 = (bf16[2,32,512]{2,1,0:T(8,128)(2,1)S(1)}, bf16[2,32,512]{2,1,0:T(8,128)(2,1)S(1)}, u32[]{:S(2)}, u32[]{:S(2)}) collective-permute-start(bf16[2,32,512]{2,1,0:T(8,128)(2,1)S(1)} %get-tuple-element.42), channel_id=1, source_target_pairs={{0,10},{1,11},{2,8},{3,9},{4,14},{5,15},{6,12},{7,13},{8,2},{9,3},... | collective-permute-start | bytes 196616 | tf_op jit(solution)/shard_map/ppermute | solution.py:396
  23.9 16.4 %collective-permute-start.6 = (bf16[2,32,512]{2,1,0:T(8,128)(2,1)S(1)}, bf16[2,32,512]{2,1,0:T(8,128)(2,1)S(1)}, u32[]{:S(2)}, u32[]{:S(2)}) collective-permute-start(bf16[2,32,512]{2,1,0:T(8,128)(2,1)S(1)} %get-tuple-element.43), channel_id=1, source_target_pairs={{0,12},{1,13},{2,14},{3,15},{4,8},{5,9},{6,10},{7,11},{8,4},{9,5},... | collective-permute-start | bytes 196616 | tf_op jit(solution)/shard_map/ppermute | solution.py:396
  27.2 13.1 %collective-permute-start.7 = (bf16[2,32,512]{2,1,0:T(8,128)(2,1)S(1)}, bf16[2,32,512]{2,1,0:T(8,128)(2,1)S(1)}, u32[]{:S(2)}, u32[]{:S(2)}) collective-permute-start(bf16[2,32,512]{2,1,0:T(8,128)(2,1)S(1)} %get-tuple-element.44), channel_id=1, source_target_pairs={{0,14},{1,15},{2,12},{3,13},{4,10},{5,11},{6,8},{7,9},{8,6},{9,7},... | collective-permute-start | bytes 196616 | tf_op jit(solution)/shard_map/ppermute | solution.py:396
  31.3 26.2 %all-to-all-start.1 = ((bf16[16,32,512]{2,1,0:T(8,128)(2,1)}), bf16[16,32,512]{2,1,0:T(8,128)(2,1)S(1)}, u32[]{:S(2)}, u32[]{:S(2)}) async-start(bf16[16,32,512]{2,1,0:T(8,128)(2,1)} %get-tuple-element.30), calls=%async_computation.1 | async-start | bytes 1048576 | tf_op jit(solution)/shard_map/all_to_all | solution.py:427
  44.1 1.6 %collective-permute-start.8 = (bf16[8,32,512]{2,1,0:T(8,128)(2,1)S(1)}, bf16[8,32,512]{2,1,0:T(8,128)(2,1)S(1)}, u32[]{:S(2)}, u32[]{:S(2)}) collective-permute-start(bf16[8,32,512]{2,1,0:T(8,128)(2,1)S(1)} %get-tuple-element.46), channel_id=1, source_target_pairs={{0,1},{1,0},{2,3},{3,2},{4,5},{5,4},{6,7},{7,6},{8,9},{9,8},{10,11... | collective-permute-start | bytes 786440 | tf_op jit(solution)/shard_map/ppermute | solution.py:390
  45.8 7.8 %collective-permute-start.9 = (bf16[2,32,512]{2,1,0:T(8,128)(2,1)S(1)}, bf16[2,32,512]{2,1,0:T(8,128)(2,1)S(1)}, u32[]{:S(2)}, u32[]{:S(2)}) collective-permute-start(bf16[2,32,512]{2,1,0:T(8,128)(2,1)S(1)} %get-tuple-element.48), channel_id=1, source_target_pairs={{0,2},{1,3},{2,0},{3,1},{4,6},{5,7},{6,4},{7,5},{8,10},{9,11},{10,... | collective-permute-start | bytes 196616 | tf_op jit(solution)/shard_map/ppermute | solution.py:396
  47.7 9.1 %collective-permute-start.10 = (bf16[2,32,512]{2,1,0:T(8,128)(2,1)S(1)}, bf16[2,32,512]{2,1,0:T(8,128)(2,1)S(1)}, u32[]{:S(2)}, u32[]{:S(2)}) collective-permute-start(bf16[2,32,512]{2,1,0:T(8,128)(2,1)S(1)} %get-tuple-element.49), channel_id=1, source_target_pairs={{0,4},{1,5},{2,6},{3,7},{4,0},{5,1},{6,2},{7,3},{8,12},{9,13},{10,... | collective-permute-start | bytes 196616 | tf_op jit(solution)/shard_map/ppermute | solution.py:396
  49.2 13.6 %collective-permute-start.11 = (bf16[2,32,512]{2,1,0:T(8,128)(2,1)S(1)}, bf16[2,32,512]{2,1,0:T(8,128)(2,1)S(1)}, u32[]{:S(2)}, u32[]{:S(2)}) collective-permute-start(bf16[2,32,512]{2,1,0:T(8,128)(2,1)S(1)} %get-tuple-element.50), channel_id=1, source_target_pairs={{0,6},{1,7},{2,4},{3,5},{4,2},{5,3},{6,0},{7,1},{8,14},{9,15},{10,... | collective-permute-start | bytes 196616 | tf_op jit(solution)/shard_map/ppermute | solution.py:396
  49.4 13.4 %collective-permute-start.12 = (bf16[2,32,512]{2,1,0:T(8,128)(2,1)S(1)}, bf16[2,32,512]{2,1,0:T(8,128)(2,1)S(1)}, u32[]{:S(2)}, u32[]{:S(2)}) collective-permute-start(bf16[2,32,512]{2,1,0:T(8,128)(2,1)S(1)} %get-tuple-element.51), channel_id=1, source_target_pairs={{0,8},{1,9},{2,10},{3,11},{4,12},{5,13},{6,14},{7,15},{8,0},{9,1},... | collective-permute-start | bytes 196616 | tf_op jit(solution)/shard_map/ppermute | solution.py:396
  52.1 13.2 %collective-permute-start.13 = (bf16[2,32,512]{2,1,0:T(8,128)(2,1)S(1)}, bf16[2,32,512]{2,1,0:T(8,128)(2,1)S(1)}, u32[]{:S(2)}, u32[]{:S(2)}) collective-permute-start(bf16[2,32,512]{2,1,0:T(8,128)(2,1)S(1)} %get-tuple-element.52), channel_id=1, source_target_pairs={{0,10},{1,11},{2,8},{3,9},{4,14},{5,15},{6,12},{7,13},{8,2},{9,3},... | collective-permute-start | bytes 196616 | tf_op jit(solution)/shard_map/ppermute | solution.py:396
  53.6 11.7 %collective-permute-start.14 = (bf16[2,32,512]{2,1,0:T(8,128)(2,1)S(1)}, bf16[2,32,512]{2,1,0:T(8,128)(2,1)S(1)}, u32[]{:S(2)}, u32[]{:S(2)}) collective-permute-start(bf16[2,32,512]{2,1,0:T(8,128)(2,1)S(1)} %get-tuple-element.53), channel_id=1, source_target_pairs={{0,12},{1,13},{2,14},{3,15},{4,8},{5,9},{6,10},{7,11},{8,4},{9,5},... | collective-permute-start | bytes 196616 | tf_op jit(solution)/shard_map/ppermute | solution.py:396
  56.9 8.5 %collective-permute-start.15 = (bf16[2,32,512]{2,1,0:T(8,128)(2,1)S(1)}, bf16[2,32,512]{2,1,0:T(8,128)(2,1)S(1)}, u32[]{:S(2)}, u32[]{:S(2)}) collective-permute-start(bf16[2,32,512]{2,1,0:T(8,128)(2,1)S(1)} %get-tuple-element.54), channel_id=1, source_target_pairs={{0,14},{1,15},{2,12},{3,13},{4,10},{5,11},{6,8},{7,9},{8,6},{9,7},... | collective-permute-start | bytes 196616 | tf_op jit(solution)/shard_map/ppermute | solution.py:396
  57.5 1.6 %copy-start.2 = (bf16[1024,1024]{1,0:T(8,128)(2,1)S(1)}, bf16[1024,1024]{1,0:T(8,128)(2,1)}, u32[]{:S(2)}) copy-start(bf16[1024,1024]{1,0:T(8,128)(2,1)} %gate_weight.1) | copy-start | bytes 6291460
  59.1 1.6 %copy-start.3 = (bf16[1024,1024]{1,0:T(8,128)(2,1)S(1)}, bf16[1024,1024]{1,0:T(8,128)(2,1)}, u32[]{:S(2)}) copy-start(bf16[1024,1024]{1,0:T(8,128)(2,1)} %weight.4) | copy-start | bytes 6291460

commit v3 on v2

--- a/solution.py
+++ b/solution.py
@@ -267,7 +267,7 @@
     plus, minus = scratch[:2]
     chip, core = place()
     copies = []
-    for slot, message in enumerate(messages):
+    for slot, message in zip(leaving_order(chips), messages):
         base = 2 * jnp.bitwise_xor(chip, slot)
         copies.append(pltpu.make_async_copy(message, gathered.at[pl.ds(base, 2)], done.at[slot]))
         copies[-1].start()
@@ -359,17 +359,27 @@
 
 
 def mix_rest_body(partial, silu, weight, *refs):
-    messages, out, gathered = refs[:-2], refs[-2], refs[-1]
+    messages, out = refs[:-4], refs[-4]
+    gathered, out_here, out_done = refs[-3:]
     devices, rest, rows = gathered.shape
     chip, core = place()
     for slot, message in enumerate(messages):
         base = 2 * jnp.bitwise_xor(chip, slot)
         gathered[base + core] = message[0]
         gathered[base + 1 - core] = message[1]
-    gated = (gathered[...].astype(f32) * silu[...]).astype(bf16).reshape(devices * rest, rows)
     used = weight[...].reshape(devices * rest, weight.shape[2])
-    total = partial[...] + jnp.dot(gated.T, used, preferred_element_type=f32)
-    out[...] = total.astype(bf16)
+    writing = []
+    for at in range(out_done.shape[0]):
+        height = rows // out_done.shape[0]
+        here = slice(height * at, height * at + height)
+        gated = (gathered[:, :, here].astype(f32) * silu[:, :, here]).astype(bf16)
+        gated = gated.reshape(devices * rest, height).T
+        total = partial[here] + jnp.dot(gated, used, preferred_element_type=f32)
+        out_here[here] = total.astype(bf16)
+        writing.append(pltpu.make_async_copy(out_here.at[here], out.at[here], out_done.at[at]))
+        writing[-1].start()
+    for copy in writing:
+        copy.wait()
 
 
 def mix_rest(partial, silu, weight, messages):
@@ -378,8 +388,12 @@
         mix_rest_body,
         out_shape=shape_of(partial.shape),
         in_specs=[VMEM] * (3 + len(messages)),
-        out_specs=VMEM,
-        scratch_shapes=[pltpu.VMEM((devices, rest, rows), bf16)],
+        out_specs=HBM,
+        scratch_shapes=[
+            pltpu.VMEM((devices, rest, rows), bf16),
+            pltpu.VMEM(partial.shape, bf16),
+            pltpu.SemaphoreType.DMA((4,)),
+        ],
         compiler_params=SMALL,
         cost_estimate=cost(2 * devices * rest * rows * weight.shape[2], 8 * rows * weight.shape[2]),
         name="mix_rest",
@@ -388,6 +402,12 @@
 
 def to_core(block, devices):
     return lax.ppermute(block, "seq", [(i, i ^ 1) for i in range(devices)])
+
+
+def leaving_order(chips):
+    half = chips // 2
+    far = sorted(range(half, chips), key=lambda slot: (slot % 2 == 0, slot))
+    return [0] + list(range(half - 1, 0, -1)) + far
 
 
 def to_chips(messages, devices):
@@ -427,6 +447,7 @@
     returned = lax.all_to_all(convolved, "seq", split_axis=0, concat_axis=0, tiled=True)
     if not splits:
         return mix_first(tokens, gate_weight, returned, out_weight)[0]
+    messages = [messages[slot] for slot in leaving_order(devices // 2)]
     keep, other = convolve_rest(lag_row, messages)
     messages = to_chips(join(keep, to_core(other, devices)), devices)
     return mix_rest(*mix_first(tokens, gate_weight, returned, out_weight), messages)

time: 67.6 us -> 65.5 us (0.969)
  starting transfers between devices: 40.8 us -> 39 us
    all_to_all x1, starting transfers between devices: 8.95 us -> 5.59 us  [body(): lax.all_to_all(convolved, 'seq', split_axis=0, concat_axis=0, tiled=True)]
    ppermute x14, starting transfers between devices: 23.5 us -> 25 us  [to_chips(): lax.ppermute(messages[slot], 'seq', [(i, i ^ 2 * slot) for i in range(dev...]
where the time goes in v3:
time: 65.5 us; the launch traced here: 65 us
  starting transfers between devices  39 us (60%)
  Pallas kernels  16.2 us (25%)
  waiting for transfers between devices  4.9 us (7%)
  local copies, waits for them, and re-layouts  4.77 us (7%)
    ppermute x14, starting transfers between devices, to_chips(): lax.ppermute(messages[slot], 'seq', [(i, i ^ 2 * slot) for i in range(dev...  25 us
    all_to_all x1, starting transfers between devices, body(): lax.all_to_all(blocks, 'seq', split_axis=0, concat_axis=0, tiled=True)  7.4 us
    all_to_all x1, starting transfers between devices, body(): lax.all_to_all(convolved, 'seq', split_axis=0, concat_axis=0, tiled=True)  5.59 us
    unnamed x8, local copies, waits for them, and re-layouts  4.77 us
    pallas_call x1, Pallas kernels, first_project(): pl.pallas_call(functools.partial(first_project_body, devices, channels, c...  4.19 us
    pallas_call x1, Pallas kernels, convolve_rest(): pl.pallas_call(rest_body, out_shape=[result] * 2, in_specs=[VMEM] + [HBM]...  3.8 us
    pallas_call x1, Pallas kernels, convolve_first(): pl.pallas_call(functools.partial(first_body, channels), out_shape=[shape_...  3.33 us
    ppermute x14, waiting for transfers between devices, to_chips(): lax.ppermute(messages[slot], 'seq', [(i, i ^ 2 * slot) for i in range(dev...  2.57 us
  transfers between devices with their start and end apart: 18, of which 3 were waited for; matrix products, arithmetic and copies ran while one was open for 0% of the time, Pallas kernels for 16%

profile of v3, /device:TPU:0, one launch (start us, length us, event | category | flops | bytes accessed | tf_op | source)
XLA Modules:
  0.0 65.0 jit_solution(5083951216682546924)
XLA Ops:
  0.0 4.2 %project_first.1 = bf16[16,136,128]{2,1,0:T(8,128)(2,1)} custom-call(bf16[512,1024]{1,0:T(8,128)(2,1)} %tokens.5, bf16[1024,1024]{1,0:T(8,128)(2,1)} %weight.5, bf16[16,1024]{1,0:T(8,128)(2,1)} %bitcast.2, f32[1,16]{1,0:T(1,128)} %bitcast.3), custom_call_target="tpu_custom_call" | custom-call | flops 1073741824 | bytes 4194304 | tf_op jit(solution)/shard_map/project_first/pallas_call | solution.py:105
  4.2 7.4 %all-to-all-start = ((bf16[16,136,128]{2,1,0:T(8,128)(2,1)}), bf16[16,136,128]{2,1,0:T(8,128)(2,1)S(1)}, u32[]{:S(2)}, u32[]{:S(2)}) async-start(bf16[16,136,128]{2,1,0:T(8,128)(2,1)} %project_first.1), calls=%async_computation | async-start | bytes 1114112 | tf_op jit(solution)/shard_map/all_to_all | solution.py:442
  11.6 1.6 %copy-done = bf16[1024,1024]{1,0:T(8,128)(2,1)S(1)} copy-done((bf16[1024,1024]{1,0:T(8,128)(2,1)S(1)}, bf16[1024,1024]{1,0:T(8,128)(2,1)}, u32[]{:S(2)}) %copy-start) | copy-done | bytes 2097176
  13.2 1.2 %project_rest.1 = (bf16[8,32,512]{2,1,0:T(8,128)(2,1)S(1)}, bf16[8,32,512]{2,1,0:T(8,128)(2,1)S(1)}) custom-call(bf16[512,1024]{1,0:T(8,128)(2,1)S(1)} %copy-done.1, bf16[1024,1024]{1,0:T(8,128)(2,1)S(1)} %copy-done), custom_call_target="tpu_custom_call" | custom-call | flops 536870912 | bytes 2097152 | tf_op jit(solution)/shard_map/project_rest/pallas_call | solution.py:138
  14.9 1.2 %collective-permute-done.other = bf16[8,32,512]{2,1,0:T(8,128)(2,1)S(1)} collective-permute-done((bf16[8,32,512]{2,1,0:T(8,128)(2,1)S(1)}, bf16[8,32,512]{2,1,0:T(8,128)(2,1)S(1)}, u32[]{:S(2)}, u32[]{:S(2)}) %collective-permute-start) | collective-permute-done | bytes 262176 | tf_op jit(solution)/shard_map/ppermute | solution.py:404
  16.1 2.9 %collective-permute-start.1 = (bf16[2,32,512]{2,1,0:T(8,128)(2,1)S(1)}, bf16[2,32,512]{2,1,0:T(8,128)(2,1)S(1)}, u32[]{:S(2)}, u32[]{:S(2)}) collective-permute-start(bf16[2,32,512]{2,1,0:T(8,128)(2,1)S(1)} %get-tuple-element.38), channel_id=1, source_target_pairs={{0,6},{1,7},{2,4},{3,5},{4,2},{5,3},{6,0},{7,1},{8,14},{9,15},{10,... | collective-permute-start | bytes 196616 | tf_op jit(solution)/shard_map/ppermute | solution.py:416
  19.7 3.7 %collective-permute-start.4 = (bf16[2,32,512]{2,1,0:T(8,128)(2,1)S(1)}, bf16[2,32,512]{2,1,0:T(8,128)(2,1)S(1)}, u32[]{:S(2)}, u32[]{:S(2)}) collective-permute-start(bf16[2,32,512]{2,1,0:T(8,128)(2,1)S(1)} %get-tuple-element.41), channel_id=1, source_target_pairs={{0,10},{1,11},{2,8},{3,9},{4,14},{5,15},{6,12},{7,13},{8,2},{9,3},... | collective-permute-start | bytes 196616 | tf_op jit(solution)/shard_map/ppermute | solution.py:416
  23.3 1.5 %collective-permute-start.5 = (bf16[2,32,512]{2,1,0:T(8,128)(2,1)S(1)}, bf16[2,32,512]{2,1,0:T(8,128)(2,1)S(1)}, u32[]{:S(2)}, u32[]{:S(2)}) collective-permute-start(bf16[2,32,512]{2,1,0:T(8,128)(2,1)S(1)} %get-tuple-element.42), channel_id=1, source_target_pairs={{0,14},{1,15},{2,12},{3,13},{4,10},{5,11},{6,8},{7,9},{8,6},{9,7},... | collective-permute-start | bytes 196616 | tf_op jit(solution)/shard_map/ppermute | solution.py:416
  24.8 4.3 %collective-permute-start.6 = (bf16[2,32,512]{2,1,0:T(8,128)(2,1)S(1)}, bf16[2,32,512]{2,1,0:T(8,128)(2,1)S(1)}, u32[]{:S(2)}, u32[]{:S(2)}) collective-permute-start(bf16[2,32,512]{2,1,0:T(8,128)(2,1)S(1)} %get-tuple-element.43), channel_id=1, source_target_pairs={{0,8},{1,9},{2,10},{3,11},{4,12},{5,13},{6,14},{7,15},{8,0},{9,1},... | collective-permute-start | bytes 196616 | tf_op jit(solution)/shard_map/ppermute | solution.py:416
  29.4 3.3 %conv_first.1 = (bf16[16,32,512]{2,1,0:T(8,128)(2,1)}, f32[1,8192]{1,0:T(1,128)S(1)}) custom-call(bf16[16,136,128]{2,1,0:T(8,128)(2,1)S(1)} %all-to-all-done.values), custom_call_target="tpu_custom_call" | custom-call | flops 1000000 | bytes 100000 | tf_op jit(solution)/shard_map/conv_first/pallas_call | solution.py:251
  32.8 5.6 %all-to-all-start.1 = ((bf16[16,32,512]{2,1,0:T(8,128)(2,1)}), bf16[16,32,512]{2,1,0:T(8,128)(2,1)S(1)}, u32[]{:S(2)}, u32[]{:S(2)}) async-start(bf16[16,32,512]{2,1,0:T(8,128)(2,1)} %get-tuple-element.30), calls=%async_computation.1 | async-start | bytes 1048576 | tf_op jit(solution)/shard_map/all_to_all | solution.py:447
  38.4 3.8 %conv_rest.1 = (bf16[8,32,512]{2,1,0:T(8,128)(2,1)S(1)}, bf16[8,32,512]{2,1,0:T(8,128)(2,1)S(1)}) custom-call(f32[1,8192]{1,0:T(1,128)S(1)} %get-tuple-element.34.lag_row, bf16[2,32,512]{2,1,0:T(8,128)(2,1)S(1)} %get-tuple-element.37.refs_0_, bf16[2,32,512]{2,1,0:T(8,128)(2,1)S(1)} %collective-permute-done.1.refs_1_, ...), custom_call_target="tpu_custom_call" | custom-call | flops 60000002048 | bytes 100000000 | tf_op jit(solution)/shard_map/conv_rest/pallas_call | solution.py:293
  42.7 1.2 %collective-permute-done.8.other = bf16[8,32,512]{2,1,0:T(8,128)(2,1)S(1)} collective-permute-done((bf16[8,32,512]{2,1,0:T(8,128)(2,1)S(1)}, bf16[8,32,512]{2,1,0:T(8,128)(2,1)S(1)}, u32[]{:S(2)}, u32[]{:S(2)}) %collective-permute-start.8) | collective-permute-done | bytes 262176 | tf_op jit(solution)/shard_map/ppermute | solution.py:404
  43.9 2.0 %collective-permute-start.9 = (bf16[2,32,512]{2,1,0:T(8,128)(2,1)S(1)}, bf16[2,32,512]{2,1,0:T(8,128)(2,1)S(1)}, u32[]{:S(2)}, u32[]{:S(2)}) collective-permute-start(bf16[2,32,512]{2,1,0:T(8,128)(2,1)S(1)} %get-tuple-element.48), channel_id=1, source_target_pairs={{0,2},{1,3},{2,0},{3,1},{4,6},{5,7},{6,4},{7,5},{8,10},{9,11},{10,... | collective-permute-start | bytes 196616 | tf_op jit(solution)/shard_map/ppermute | solution.py:416
  45.9 1.5 %collective-permute-start.10 = (bf16[2,32,512]{2,1,0:T(8,128)(2,1)S(1)}, bf16[2,32,512]{2,1,0:T(8,128)(2,1)S(1)}, u32[]{:S(2)}, u32[]{:S(2)}) collective-permute-start(bf16[2,32,512]{2,1,0:T(8,128)(2,1)S(1)} %get-tuple-element.49), channel_id=1, source_target_pairs={{0,4},{1,5},{2,6},{3,7},{4,0},{5,1},{6,2},{7,3},{8,12},{9,13},{10,... | collective-permute-start | bytes 196616 | tf_op jit(solution)/shard_map/ppermute | solution.py:416
  47.5 2.8 %collective-permute-start.12 = (bf16[2,32,512]{2,1,0:T(8,128)(2,1)S(1)}, bf16[2,32,512]{2,1,0:T(8,128)(2,1)S(1)}, u32[]{:S(2)}, u32[]{:S(2)}) collective-permute-start(bf16[2,32,512]{2,1,0:T(8,128)(2,1)S(1)} %get-tuple-element.51), channel_id=1, source_target_pairs={{0,8},{1,9},{2,10},{3,11},{4,12},{5,13},{6,14},{7,15},{8,0},{9,1},... | collective-permute-start | bytes 196616 | tf_op jit(solution)/shard_map/ppermute | solution.py:416
  50.2 1.5 %collective-permute-start.13 = (bf16[2,32,512]{2,1,0:T(8,128)(2,1)S(1)}, bf16[2,32,512]{2,1,0:T(8,128)(2,1)S(1)}, u32[]{:S(2)}, u32[]{:S(2)}) collective-permute-start(bf16[2,32,512]{2,1,0:T(8,128)(2,1)S(1)} %get-tuple-element.52), channel_id=1, source_target_pairs={{0,10},{1,11},{2,8},{3,9},{4,14},{5,15},{6,12},{7,13},{8,2},{9,3},... | collective-permute-start | bytes 196616 | tf_op jit(solution)/shard_map/ppermute | solution.py:416
  51.7 3.3 %collective-permute-start.14 = (bf16[2,32,512]{2,1,0:T(8,128)(2,1)S(1)}, bf16[2,32,512]{2,1,0:T(8,128)(2,1)S(1)}, u32[]{:S(2)}, u32[]{:S(2)}) collective-permute-start(bf16[2,32,512]{2,1,0:T(8,128)(2,1)S(1)} %get-tuple-element.53), channel_id=1, source_target_pairs={{0,12},{1,13},{2,14},{3,15},{4,8},{5,9},{6,10},{7,11},{8,4},{9,5},... | collective-permute-start | bytes 196616 | tf_op jit(solution)/shard_map/ppermute | solution.py:416
  55.0 0.6 collective-permute-start.15
  55.6 1.6 %copy-done.2 = bf16[1024,1024]{1,0:T(8,128)(2,1)S(1)} copy-done((bf16[1024,1024]{1,0:T(8,128)(2,1)S(1)}, bf16[1024,1024]{1,0:T(8,128)(2,1)}, u32[]{:S(2)}) %copy-start.2) | copy-done | bytes 2097176
  57.2 1.6 %copy-done.3 = bf16[1024,1024]{1,0:T(8,128)(2,1)S(1)} copy-done((bf16[1024,1024]{1,0:T(8,128)(2,1)S(1)}, bf16[1024,1024]{1,0:T(8,128)(2,1)}, u32[]{:S(2)}) %copy-start.3) | copy-done | bytes 2097176
  58.8 2.1 %mix_first.1 = (f32[512,1024]{1,0:T(8,128)S(1)}, f32[16,32,512]{2,1,0:T(8,128)S(1)}, bf16[16,32,1024]{2,1,0:T(8,128)(2,1)S(1)}) custom-call(bf16[512,1024]{1,0:T(8,128)(2,1)S(1)} %copy-done.1, bf16[1024,1024]{1,0:T(8,128)(2,1)S(1)} %copy-done.2, bf16[16,32,512]{2,1,0:T(8,128)(2,1)S(1)} %all-to-all-done.1.conv, bf16[1024,1024]{1,0:T(8,128)(2,1)S(1)} %copy-done.3), custom_call_target="tpu_custom_call" | custom-call | flops 2147483648 | bytes 4194304 | tf_op jit(solution)/shard_map/mix_first/pallas_call | solution.py:350
  60.9 2.5 %collective-permute-done.13.refs_5_ = bf16[2,32,512]{2,1,0:T(8,128)(2,1)S(1)} collective-permute-done((bf16[2,32,512]{2,1,0:T(8,128)(2,1)S(1)}, bf16[2,32,512]{2,1,0:T(8,128)(2,1)S(1)}, u32[]{:S(2)}, u32[]{:S(2)}) %collective-permute-start.13) | collective-permute-done | bytes 65568 | tf_op jit(solution)/shard_map/ppermute | solution.py:416
  63.5 1.6 %mix_rest.1 = bf16[512,1024]{1,0:T(8,128)(2,1)} custom-call(f32[512,1024]{1,0:T(8,128)S(1)} %get-tuple-element.31.partial, f32[16,32,512]{2,1,0:T(8,128)S(1)} %get-tuple-element.32.silu, bf16[16,32,1024]{2,1,0:T(8,128)(2,1)S(1)} %get-tuple-element.33.weight, bf16[2,32,512]{2,1,0:T(8,128)(2,1)S(1)} %get-tuple-element.47.refs_0_, ...), custom_call_target="tpu_custom_call" | custom-call | flops 536870912 | bytes 4194304 | tf_op jit(solution)/shard_map/mix_rest/pallas_call | solution.py:387
  (28 shorter events, 2.2 us)
Async XLA Ops:
  0.0 11.6 %copy-start.1 = (bf16[512,1024]{1,0:T(8,128)(2,1)S(1)}, bf16[512,1024]{1,0:T(8,128)(2,1)}, u32[]{:S(2)}) copy-start(bf16[512,1024]{1,0:T(8,128)(2,1)} %tokens.5) | copy-start | bytes 3145732
  4.2 25.2 %all-to-all-start = ((bf16[16,136,128]{2,1,0:T(8,128)(2,1)}), bf16[16,136,128]{2,1,0:T(8,128)(2,1)S(1)}, u32[]{:S(2)}, u32[]{:S(2)}) async-start(bf16[16,136,128]{2,1,0:T(8,128)(2,1)} %project_first.1), calls=%async_computation | async-start | bytes 1114112 | tf_op jit(solution)/shard_map/all_to_all | solution.py:442
  11.6 1.6 %copy-start = (bf16[1024,1024]{1,0:T(8,128)(2,1)S(1)}, bf16[1024,1024]{1,0:T(8,128)(2,1)}, u32[]{:S(2)}) copy-start(bf16[1024,1024]{1,0:T(8,128)(2,1)} %weight.5) | copy-start | bytes 6291460
  14.4 1.6 %collective-permute-start = (bf16[8,32,512]{2,1,0:T(8,128)(2,1)S(1)}, bf16[8,32,512]{2,1,0:T(8,128)(2,1)S(1)}, u32[]{:S(2)}, u32[]{:S(2)}) collective-permute-start(bf16[8,32,512]{2,1,0:T(8,128)(2,1)S(1)} %get-tuple-element.36), channel_id=1, source_target_pairs={{0,1},{1,0},{2,3},{3,2},{4,5},{5,4},{6,7},{7,6},{8,9},{9,8},{10,11... | collective-permute-start | bytes 786440 | tf_op jit(solution)/shard_map/ppermute | solution.py:404
  16.1 8.7 %collective-permute-start.1 = (bf16[2,32,512]{2,1,0:T(8,128)(2,1)S(1)}, bf16[2,32,512]{2,1,0:T(8,128)(2,1)S(1)}, u32[]{:S(2)}, u32[]{:S(2)}) collective-permute-start(bf16[2,32,512]{2,1,0:T(8,128)(2,1)S(1)} %get-tuple-element.38), channel_id=1, source_target_pairs={{0,6},{1,7},{2,4},{3,5},{4,2},{5,3},{6,0},{7,1},{8,14},{9,15},{10,... | collective-permute-start | bytes 196616 | tf_op jit(solution)/shard_map/ppermute | solution.py:416
  19.0 10.2 %collective-permute-start.2 = (bf16[2,32,512]{2,1,0:T(8,128)(2,1)S(1)}, bf16[2,32,512]{2,1,0:T(8,128)(2,1)S(1)}, u32[]{:S(2)}, u32[]{:S(2)}) collective-permute-start(bf16[2,32,512]{2,1,0:T(8,128)(2,1)S(1)} %get-tuple-element.39), channel_id=1, source_target_pairs={{0,4},{1,5},{2,6},{3,7},{4,0},{5,1},{6,2},{7,3},{8,12},{9,13},{10,... | collective-permute-start | bytes 196616 | tf_op jit(solution)/shard_map/ppermute | solution.py:416
  19.5 18.9 %collective-permute-start.3 = (bf16[2,32,512]{2,1,0:T(8,128)(2,1)S(1)}, bf16[2,32,512]{2,1,0:T(8,128)(2,1)S(1)}, u32[]{:S(2)}, u32[]{:S(2)}) collective-permute-start(bf16[2,32,512]{2,1,0:T(8,128)(2,1)S(1)} %get-tuple-element.40), channel_id=1, source_target_pairs={{0,2},{1,3},{2,0},{3,1},{4,6},{5,7},{6,4},{7,5},{8,10},{9,11},{10,... | collective-permute-start | bytes 196616 | tf_op jit(solution)/shard_map/ppermute | solution.py:416
  19.7 18.7 %collective-permute-start.4 = (bf16[2,32,512]{2,1,0:T(8,128)(2,1)S(1)}, bf16[2,32,512]{2,1,0:T(8,128)(2,1)S(1)}, u32[]{:S(2)}, u32[]{:S(2)}) collective-permute-start(bf16[2,32,512]{2,1,0:T(8,128)(2,1)S(1)} %get-tuple-element.41), channel_id=1, source_target_pairs={{0,10},{1,11},{2,8},{3,9},{4,14},{5,15},{6,12},{7,13},{8,2},{9,3},... | collective-permute-start | bytes 196616 | tf_op jit(solution)/shard_map/ppermute | solution.py:416
  23.3 15.0 %collective-permute-start.5 = (bf16[2,32,512]{2,1,0:T(8,128)(2,1)S(1)}, bf16[2,32,512]{2,1,0:T(8,128)(2,1)S(1)}, u32[]{:S(2)}, u32[]{:S(2)}) collective-permute-start(bf16[2,32,512]{2,1,0:T(8,128)(2,1)S(1)} %get-tuple-element.42), channel_id=1, source_target_pairs={{0,14},{1,15},{2,12},{3,13},{4,10},{5,11},{6,8},{7,9},{8,6},{9,7},... | collective-permute-start | bytes 196616 | tf_op jit(solution)/shard_map/ppermute | solution.py:416
  24.8 13.6 %collective-permute-start.6 = (bf16[2,32,512]{2,1,0:T(8,128)(2,1)S(1)}, bf16[2,32,512]{2,1,0:T(8,128)(2,1)S(1)}, u32[]{:S(2)}, u32[]{:S(2)}) collective-permute-start(bf16[2,32,512]{2,1,0:T(8,128)(2,1)S(1)} %get-tuple-element.43), channel_id=1, source_target_pairs={{0,8},{1,9},{2,10},{3,11},{4,12},{5,13},{6,14},{7,15},{8,0},{9,1},... | collective-permute-start | bytes 196616 | tf_op jit(solution)/shard_map/ppermute | solution.py:416
  29.1 9.3 %collective-permute-start.7 = (bf16[2,32,512]{2,1,0:T(8,128)(2,1)S(1)}, bf16[2,32,512]{2,1,0:T(8,128)(2,1)S(1)}, u32[]{:S(2)}, u32[]{:S(2)}) collective-permute-start(bf16[2,32,512]{2,1,0:T(8,128)(2,1)S(1)} %get-tuple-element.44), channel_id=1, source_target_pairs={{0,12},{1,13},{2,14},{3,15},{4,8},{5,9},{6,10},{7,11},{8,4},{9,5},... | collective-permute-start | bytes 196616 | tf_op jit(solution)/shard_map/ppermute | solution.py:416
  32.8 22.8 %all-to-all-start.1 = ((bf16[16,32,512]{2,1,0:T(8,128)(2,1)}), bf16[16,32,512]{2,1,0:T(8,128)(2,1)S(1)}, u32[]{:S(2)}, u32[]{:S(2)}) async-start(bf16[16,32,512]{2,1,0:T(8,128)(2,1)} %get-tuple-element.30), calls=%async_computation.1 | async-start | bytes 1048576 | tf_op jit(solution)/shard_map/all_to_all | solution.py:447
  42.2 1.6 %collective-permute-start.8 = (bf16[8,32,512]{2,1,0:T(8,128)(2,1)S(1)}, bf16[8,32,512]{2,1,0:T(8,128)(2,1)S(1)}, u32[]{:S(2)}, u32[]{:S(2)}) collective-permute-start(bf16[8,32,512]{2,1,0:T(8,128)(2,1)S(1)} %get-tuple-element.46), channel_id=1, source_target_pairs={{0,1},{1,0},{2,3},{3,2},{4,5},{5,4},{6,7},{7,6},{8,9},{9,8},{10,11... | collective-permute-start | bytes 786440 | tf_op jit(solution)/shard_map/ppermute | solution.py:404
  43.9 7.8 %collective-permute-start.9 = (bf16[2,32,512]{2,1,0:T(8,128)(2,1)S(1)}, bf16[2,32,512]{2,1,0:T(8,128)(2,1)S(1)}, u32[]{:S(2)}, u32[]{:S(2)}) collective-permute-start(bf16[2,32,512]{2,1,0:T(8,128)(2,1)S(1)} %get-tuple-element.48), channel_id=1, source_target_pairs={{0,2},{1,3},{2,0},{3,1},{4,6},{5,7},{6,4},{7,5},{8,10},{9,11},{10,... | collective-permute-start | bytes 196616 | tf_op jit(solution)/shard_map/ppermute | solution.py:416
  45.9 9.1 %collective-permute-start.10 = (bf16[2,32,512]{2,1,0:T(8,128)(2,1)S(1)}, bf16[2,32,512]{2,1,0:T(8,128)(2,1)S(1)}, u32[]{:S(2)}, u32[]{:S(2)}) collective-permute-start(bf16[2,32,512]{2,1,0:T(8,128)(2,1)S(1)} %get-tuple-element.49), channel_id=1, source_target_pairs={{0,4},{1,5},{2,6},{3,7},{4,0},{5,1},{6,2},{7,3},{8,12},{9,13},{10,... | collective-permute-start | bytes 196616 | tf_op jit(solution)/shard_map/ppermute | solution.py:416
  47.3 13.6 %collective-permute-start.11 = (bf16[2,32,512]{2,1,0:T(8,128)(2,1)S(1)}, bf16[2,32,512]{2,1,0:T(8,128)(2,1)S(1)}, u32[]{:S(2)}, u32[]{:S(2)}) collective-permute-start(bf16[2,32,512]{2,1,0:T(8,128)(2,1)S(1)} %get-tuple-element.50), channel_id=1, source_target_pairs={{0,6},{1,7},{2,4},{3,5},{4,2},{5,3},{6,0},{7,1},{8,14},{9,15},{10,... | collective-permute-start | bytes 196616 | tf_op jit(solution)/shard_map/ppermute | solution.py:416
  47.5 13.4 %collective-permute-start.12 = (bf16[2,32,512]{2,1,0:T(8,128)(2,1)S(1)}, bf16[2,32,512]{2,1,0:T(8,128)(2,1)S(1)}, u32[]{:S(2)}, u32[]{:S(2)}) collective-permute-start(bf16[2,32,512]{2,1,0:T(8,128)(2,1)S(1)} %get-tuple-element.51), channel_id=1, source_target_pairs={{0,8},{1,9},{2,10},{3,11},{4,12},{5,13},{6,14},{7,15},{8,0},{9,1},... | collective-permute-start | bytes 196616 | tf_op jit(solution)/shard_map/ppermute | solution.py:416
  50.2 13.2 %collective-permute-start.13 = (bf16[2,32,512]{2,1,0:T(8,128)(2,1)S(1)}, bf16[2,32,512]{2,1,0:T(8,128)(2,1)S(1)}, u32[]{:S(2)}, u32[]{:S(2)}) collective-permute-start(bf16[2,32,512]{2,1,0:T(8,128)(2,1)S(1)} %get-tuple-element.52), channel_id=1, source_target_pairs={{0,10},{1,11},{2,8},{3,9},{4,14},{5,15},{6,12},{7,13},{8,2},{9,3},... | collective-permute-start | bytes 196616 | tf_op jit(solution)/shard_map/ppermute | solution.py:416
  51.7 11.7 %collective-permute-start.14 = (bf16[2,32,512]{2,1,0:T(8,128)(2,1)S(1)}, bf16[2,32,512]{2,1,0:T(8,128)(2,1)S(1)}, u32[]{:S(2)}, u32[]{:S(2)}) collective-permute-start(bf16[2,32,512]{2,1,0:T(8,128)(2,1)S(1)} %get-tuple-element.53), channel_id=1, source_target_pairs={{0,12},{1,13},{2,14},{3,15},{4,8},{5,9},{6,10},{7,11},{8,4},{9,5},... | collective-permute-start | bytes 196616 | tf_op jit(solution)/shard_map/ppermute | solution.py:416
  55.0 8.5 %collective-permute-start.15 = (bf16[2,32,512]{2,1,0:T(8,128)(2,1)S(1)}, bf16[2,32,512]{2,1,0:T(8,128)(2,1)S(1)}, u32[]{:S(2)}, u32[]{:S(2)}) collective-permute-start(bf16[2,32,512]{2,1,0:T(8,128)(2,1)S(1)} %get-tuple-element.54), channel_id=1, source_target_pairs={{0,14},{1,15},{2,12},{3,13},{4,10},{5,11},{6,8},{7,9},{8,6},{9,7},... | collective-permute-start | bytes 196616 | tf_op jit(solution)/shard_map/ppermute | solution.py:416
  55.6 1.6 %copy-start.2 = (bf16[1024,1024]{1,0:T(8,128)(2,1)S(1)}, bf16[1024,1024]{1,0:T(8,128)(2,1)}, u32[]{:S(2)}) copy-start(bf16[1024,1024]{1,0:T(8,128)(2,1)} %gate_weight.1) | copy-start | bytes 6291460
  57.2 1.6 %copy-start.3 = (bf16[1024,1024]{1,0:T(8,128)(2,1)S(1)}, bf16[1024,1024]{1,0:T(8,128)(2,1)}, u32[]{:S(2)}) copy-start(bf16[1024,1024]{1,0:T(8,128)(2,1)} %weight.4) | copy-start | bytes 6291460
